TPU v7x, 512 devices: a whole 4x4x16 slice. The times are simulated.
512 devices in a mesh: frame: 64 (over z, x), head: 4 (over y_hi, core), dp: 2 (over y_lo).
Axes of the slice: x: 4, y: 4 (y_hi: 2, y_lo: 2; y = y_hi * 2 + y_lo), z: 16, core: 2. Of those that a mesh axis runs over, the one named last changes fastest.
Arguments:
- inputs: bfloat16 [128, 128, 1152], P(('dp', 'frame')), parts along dimension 0, may hold values from -6 to 6
- modulation: float32 [6, 1152], P('dp'), parts along dimension 0, may hold values from -3 to 3
- qkv_weight: bfloat16 [3, 1152, 1152], P(None, 'frame', 'head'), may hold values from -0.1875 to 0.1875
- proj_weight: bfloat16 [1152, 1152], P('head', 'frame'), may hold values from -0.1875 to 0.1875
- q_gain: float32 [72], replicated, may hold values from 0.5 to 10
- k_gain: float32 [72], replicated, may hold values from 0.5 to 10
- cotangent: bfloat16 [128, 128, 1152], P(('dp', 'frame')), parts along dimension 0, may hold values from -16 to 16
Outputs:
- output: bfloat16 [128, 128, 1152], P(('dp', 'frame')), parts along dimension 0
- input_grad: bfloat16 [128, 128, 1152], P(('dp', 'frame')), parts along dimension 0
- proj_grad: float32 [2304, 1152], P(('dp', 'head'), 'frame'), parts along dimension 0
There are 2 independent parts, one for each index of `dp`. A program takes and returns all parts, laid end to end along the dimension named above; an argument that names none is the same for every part. Nothing has to cross between parts.
All inputs are finite; a program needn't handle non-finite values.
Results may differ from a plain program's by a relative error of at most 0.015.
The roundings to bfloat16 on the way count: a program that leaves them out, or rounds other values in their place, can miss the bound.
Values may be sent and summed in bfloat16 or wider, within the bound.
A program may use at most 64 MiB of HBM per device.

v0:
```python
import jax
import jax.numpy as jnp
from jax import lax
from jax.sharding import PartitionSpec as P


def head_norm(raw_part, gain_vec):
    inv_root = 1.0 / jnp.sqrt(jnp.mean(raw_part * raw_part, axis=-1, keepdims=True) + 1e-06)
    return ((raw_part * inv_root * gain_vec).astype(jnp.bfloat16), inv_root)


def head_norm_back(raw_part, inv_root, gain_vec, d_normed):
    scaled = gain_vec * d_normed.astype(jnp.float32)
    inner = jnp.mean(raw_part * scaled, axis=-1, keepdims=True)
    return (inv_root * scaled - raw_part * inv_root**3 * inner).astype(jnp.bfloat16)


def per_device(inputs, modulation, qkv_weight, proj_weight, q_gain, k_gain, cotangent):
    frames_here, spatial_n, width = inputs.shape
    tok_rows = frames_here * spatial_n
    head_dim = q_gain.shape[0]
    local_cols = qkv_weight.shape[2]
    local_heads = local_cols // head_dim
    inputs_f = inputs.reshape(tok_rows, width).astype(jnp.float32)
    shift_vec, scale_vec, gate_vec = (modulation[0], modulation[1], modulation[2])
    center = jnp.mean(inputs_f, axis=1, keepdims=True)
    centered = inputs_f - center
    rstd_col = 1.0 / jnp.sqrt(jnp.mean(centered * centered, axis=1, keepdims=True) + 1e-06)
    normed = centered * rstd_col
    hidden_in = (normed * (1.0 + scale_vec) + shift_vec).astype(jnp.bfloat16)
    columns = hidden_in
    raw_proj = jnp.einsum(
        "rn,wne->wre",
        columns,
        lax.all_gather(qkv_weight, "frame", axis=1, tiled=True),
        preferred_element_type=jnp.float32,
    )
    raw_query = raw_proj[0].reshape(tok_rows, local_heads, head_dim)
    raw_key = raw_proj[1].reshape(tok_rows, local_heads, head_dim)
    query, root_q = head_norm(raw_query, q_gain)
    key_n, root_k = head_norm(raw_key, k_gain)
    value = raw_proj[2].astype(jnp.bfloat16)
    stacked = jnp.stack(
        [query.reshape(tok_rows, local_cols), key_n.reshape(tok_rows, local_cols), value]
    )
    stacked = stacked.reshape(3, frames_here, spatial_n, local_cols)
    spread = lax.all_to_all(stacked, "frame", split_axis=2, concat_axis=1, tiled=True)
    all_frames = spread.shape[1]
    positions = spread.shape[2]
    spread = spread.reshape(3, all_frames, positions, local_heads, head_dim)
    query_s, key_s, value_s = (spread[0], spread[1], spread[2])
    factor = 1.0 / jnp.sqrt(jnp.float32(head_dim))
    scores = (
        jnp.einsum("fphd,gphd->phfg", query_s, key_s, preferred_element_type=jnp.float32) * factor
    )
    peak = jnp.max(scores, axis=-1, keepdims=True)
    expo = jnp.exp(scores - peak)
    probs = expo / jnp.sum(expo, axis=-1, keepdims=True)
    probs_b = probs.astype(jnp.bfloat16)
    attended_s = jnp.einsum(
        "phfg,gphd->fphd", probs_b, value_s, preferred_element_type=jnp.float32
    ).astype(jnp.bfloat16)
    attended_s = attended_s.reshape(all_frames, positions, local_cols)
    attended = lax.all_to_all(attended_s, "frame", split_axis=0, concat_axis=1, tiled=True).reshape(
        tok_rows, local_cols
    )
    partial_branch = jnp.dot(
        attended,
        lax.all_gather(proj_weight, "frame", axis=1, tiled=True),
        preferred_element_type=jnp.float32,
    )
    branch = lax.psum(partial_branch, "head")
    output = (inputs_f + gate_vec * branch).astype(jnp.bfloat16)
    d_out = cotangent.reshape(tok_rows, width).astype(jnp.float32)
    d_branch = (gate_vec * d_out).astype(jnp.bfloat16)
    grad_term = lax.dot_general(
        attended, d_branch, (((0,), (0,)), ((), ())), preferred_element_type=jnp.float32
    )
    proj_grad = lax.psum_scatter(grad_term, "frame", scatter_dimension=1, tiled=True)
    columns = d_branch
    d_att = lax.dot_general(
        columns,
        lax.all_gather(proj_weight, "frame", axis=1, tiled=True),
        (((1,), (1,)), ((), ())),
        preferred_element_type=jnp.float32,
    )
    d_att = d_att.astype(jnp.bfloat16).reshape(frames_here, spatial_n, local_cols)
    d_att_s = lax.all_to_all(d_att, "frame", split_axis=1, concat_axis=0, tiled=True)
    d_att_s = d_att_s.reshape(all_frames, positions, local_heads, head_dim)
    d_value = jnp.einsum(
        "phfg,fphd->gphd", probs_b, d_att_s, preferred_element_type=jnp.float32
    ).astype(jnp.bfloat16)
    d_probs = jnp.einsum("fphd,gphd->phfg", d_att_s, value_s, preferred_element_type=jnp.float32)
    d_scores = (
        probs * (d_probs - jnp.sum(probs * d_probs, axis=-1, keepdims=True)) * factor
    ).astype(jnp.bfloat16)
    d_query = jnp.einsum(
        "phfg,gphd->fphd", d_scores, key_s, preferred_element_type=jnp.float32
    ).astype(jnp.bfloat16)
    d_key = jnp.einsum(
        "phfg,fphd->gphd", d_scores, query_s, preferred_element_type=jnp.float32
    ).astype(jnp.bfloat16)
    d_stack = jnp.stack([d_query, d_key, d_value]).reshape(3, all_frames, positions, local_cols)
    d_back = lax.all_to_all(d_stack, "frame", split_axis=1, concat_axis=2, tiled=True)
    d_back = d_back.reshape(3, tok_rows, local_heads, head_dim)
    d_raw_q = head_norm_back(raw_query, root_q, q_gain, d_back[0])
    d_raw_k = head_norm_back(raw_key, root_k, k_gain, d_back[1])
    d_raw = jnp.stack(
        [
            d_raw_q.reshape(tok_rows, local_cols),
            d_raw_k.reshape(tok_rows, local_cols),
            d_back[2].reshape(tok_rows, local_cols),
        ]
    )
    partial_hidden = jnp.einsum(
        "wre,wne->rn",
        d_raw,
        lax.all_gather(qkv_weight, "frame", axis=1, tiled=True),
        preferred_element_type=jnp.float32,
    )
    d_hidden = lax.psum(partial_hidden, "head")
    d_normed = d_hidden * (1.0 + scale_vec)
    d_in = rstd_col * (
        d_normed
        - jnp.mean(d_normed, axis=1, keepdims=True)
        - normed * jnp.mean(d_normed * normed, axis=1, keepdims=True)
    )
    input_grad = (d_out + d_in).astype(jnp.bfloat16)
    return (
        output.reshape(frames_here, spatial_n, width),
        input_grad.reshape(frames_here, spatial_n, width),
        proj_grad,
    )


def solution(mesh):
    return jax.shard_map(
        per_device,
        mesh=mesh,
        in_specs=(
            P(("dp", "frame"), None, None),
            P("dp", None),
            P(None, "frame", "head"),
            P("head", "frame"),
            P(),
            P(),
            P(("dp", "frame"), None, None),
        ),
        out_specs=(
            P(("dp", "frame"), None, None),
            P(("dp", "frame"), None, None),
            P(("dp", "head"), "frame"),
        ),
        check_vma=False,
    )
```

profile of v0, /device:TPU:1, one launch (start us, length us, event | category | flops | bytes accessed | tf_op | source)
XLA Modules:
  0.0 582.5 jit_solution(12448579469147794383)
XLA Ops:
  7.2 1.5 copy.81
  8.8 87.0 %all-gather = bf16[64,18,288]{2,1,0:T(8,128)(2,1)S(1)} all-gather(bf16[1,18,288]{2,1,0:T(8,128)(2,1)} %bitcast.152), channel_id=1, replica_groups=mesh['frame'=64,'head'=4,'dp'=2] {'frame'}, dimensions={0}, use_global_device_ids=true | all-gather | bytes 673920 | tf_op jit(solution)/shard_map/all_gather | solution.py:69
  97.5 1.3 reduce.15
  99.5 8.3 %all-to-all-start.2 = ((bf16[64,2,288]{2,1,0:T(2,128)(2,1)}), bf16[64,2,288]{2,1,0:T(2,128)(2,1)S(1)}, u32[]{:S(2)}, u32[]{:S(2)}) async-start(bf16[64,2,288]{2,1,0:T(2,128)(2,1)} %reshape.300), calls=%async_computation.2 | async-start | bytes 196608 | tf_op jit(solution)/shard_map/all_to_all | solution.py:88
  108.3 45.9 %all-gather.3.cloned.1.call-done = bf16[3,1152,288]{2,0,1:T(4,128)(2,1)} async-done(((bf16[3,18,288]{2,0,1:T(4,128)(2,1)}), bf16[3,1152,288]{2,0,1:T(4,128)(2,1)}) %all-gather.3.cloned.1.call-update) | async-done | bytes 1990672 | tf_op jit(solution)/shard_map/all_gather | solution.py:35
  154.2 3.1 fusion.5
  158.6 10.0 %all-to-all-start = ((bf16[3,1,128,288]{3,0,1,2:T(4,128)(2,1)}), bf16[3,1,128,288]{3,0,1,2:T(4,128)(2,1)S(1)}, u32[]{:S(2)}, u32[]{:S(2)}) async-start(bf16[3,1,128,288]{3,0,1,2:T(4,128)(2,1)} %copy.83), calls=%async_computation | async-start | bytes 786432 | tf_op jit(solution)/shard_map/all_to_all | solution.py:47
  169.4 18.7 %all-to-all-done = bf16[3,1,128,288]{3,0,1,2:T(4,128)(2,1)S(1)} async-done(((bf16[3,1,128,288]{3,0,1,2:T(4,128)(2,1)}), bf16[3,1,128,288]{3,0,1,2:T(4,128)(2,1)S(1)}, u32[]{:S(2)}, u32[]{:S(2)}) %all-to-all-start) | async-done | bytes 221216 | tf_op jit(solution)/shard_map/all_to_all | solution.py:47
  188.1 1.5 slice_reduce_fusion.1
  191.2 1.3 fusion.15
  192.5 1.3 fusion.16
  195.7 5.4 all-to-all-start.1
  202.8 12.8 %all-to-all-done.1 = bf16[64,2,288]{2,1,0:T(2,128)(2,1)S(1)} async-done(((bf16[64,2,288]{2,1,0:T(2,128)(2,1)}), bf16[64,2,288]{2,1,0:T(2,128)(2,1)S(1)}, u32[]{:S(2)}, u32[]{:S(2)}) %all-to-all-start.1) | async-done | bytes 73760 | tf_op jit(solution)/shard_map/all_to_all | solution.py:64
  215.6 4.6 all-to-all-start.3
  220.6 1.7 fusion.43
  222.4 1.3 fusion.119
  223.7 14.7 %all-to-all-done.3 = bf16[3,64,2,288]{3,2,0,1:T(2,128)(2,1)S(1)} async-done(((bf16[3,64,2,288]{3,2,0,1:T(2,128)(2,1)}), bf16[3,64,2,288]{3,2,0,1:T(2,128)(2,1)S(1)}, u32[]{:S(2)}, u32[]{:S(2)}) %all-to-all-start.3) | async-done | bytes 221216 | tf_op jit(solution)/shard_map/all_to_all | solution.py:104
  241.0 3.8 convolution_bitcast_fusion
  244.8 1.3 dynamic-slice
  246.7 256.3 %all-reduce.5.cloned.1.call-done = f32[288,1152]{0,1:T(8,128)} async-done(((f32[288,1152]{0,1:T(8,128)}), f32[288,1152]{0,1:T(8,128)}) %all-reduce.5.cloned.1.call-update) | async-done | bytes 1327120
  503.1 1.4 constant_dynamic-slice_fusion
  504.5 67.9 %all-reduce.7.cloned.1.call-done = (f32[128,1152]{1,0:T(8,128)}, f32[128,1152]{1,0:T(8,128)}) async-done(((f32[128,1152]{1,0:T(8,128)}, f32[128,1152]{1,0:T(8,128)}), (f32[128,1152]{1,0:T(8,128)}, f32[128,1152]{1,0:T(8,128)})) %all-reduce.7.cloned.1.call-update) | async-done | bytes 1179664 | tf_op jit(solution)/shard_map/psum | solution.py:72
  572.4 1.3 multiply_reduce_fusion
  573.7 2.3 fusion.45
  (80 shorter events, 13.1 us)
Async XLA Ops:
  7.2 89.2 %copy-start.2 = (f32[3,1152]{1,0:T(4,128)S(1)}, f32[3,1152]{1,0:T(4,128)}, u32[]{:S(2)}) copy-start(f32[3,1152]{1,0:T(4,128)} %param.8) | copy-start | bytes 41476
  7.2 89.2 %copy-start.1 = (bf16[1,128,1152]{2,1,0:T(8,128)(2,1)S(1)}, bf16[1,128,1152]{2,1,0:T(8,128)(2,1)}, u32[]{:S(2)}) copy-start(bf16[1,128,1152]{2,1,0:T(8,128)(2,1)} %param.13) | copy-start | bytes 884740
  7.2 147.0 %all-gather.3.cloned.1.call-start = ((), (), s32[]{:S(2)}) async-start(), calls=%async_computation.4 | async-start | bytes 3594240 | tf_op jit(solution)/shard_map/all_gather | solution.py:35
  8.7 99.0 %copy-start.4 = (f32[72]{0:T(128)S(1)}, f32[72]{0:T(128)}, u32[]{:S(2)}) copy-start(f32[72]{0:T(128)} %param.11) | copy-start | bytes 868
  8.8 99.1 %copy-start.3 = (f32[72]{0:T(128)S(1)}, f32[72]{0:T(128)}, u32[]{:S(2)}) copy-start(f32[72]{0:T(128)} %param.12) | copy-start | bytes 868
  8.8 99.2 %copy-start = (bf16[1,128,1152]{2,1,0:T(8,128)(2,1)S(1)}, bf16[1,128,1152]{2,1,0:T(8,128)(2,1)}, u32[]{:S(2)}) copy-start(bf16[1,128,1152]{2,1,0:T(8,128)(2,1)} %param.7) | copy-start | bytes 884740
  99.5 59.1 %all-to-all-start.2 = ((bf16[64,2,288]{2,1,0:T(2,128)(2,1)}), bf16[64,2,288]{2,1,0:T(2,128)(2,1)S(1)}, u32[]{:S(2)}, u32[]{:S(2)}) async-start(bf16[64,2,288]{2,1,0:T(2,128)(2,1)} %reshape.300), calls=%async_computation.2 | async-start | bytes 196608 | tf_op jit(solution)/shard_map/all_to_all | solution.py:88
  158.6 29.5 %all-to-all-start = ((bf16[3,1,128,288]{3,0,1,2:T(4,128)(2,1)}), bf16[3,1,128,288]{3,0,1,2:T(4,128)(2,1)S(1)}, u32[]{:S(2)}, u32[]{:S(2)}) async-start(bf16[3,1,128,288]{3,0,1,2:T(4,128)(2,1)} %copy.83), calls=%async_computation | async-start | bytes 786432 | tf_op jit(solution)/shard_map/all_to_all | solution.py:47
  195.7 19.9 %all-to-all-start.1 = ((bf16[64,2,288]{2,1,0:T(2,128)(2,1)}), bf16[64,2,288]{2,1,0:T(2,128)(2,1)S(1)}, u32[]{:S(2)}, u32[]{:S(2)}) async-start(bf16[64,2,288]{2,1,0:T(2,128)(2,1)} %reshape.291), calls=%async_computation.1 | async-start | bytes 196608 | tf_op jit(solution)/shard_map/all_to_all | solution.py:64
  215.6 22.8 %all-to-all-start.3 = ((bf16[3,64,2,288]{3,2,0,1:T(2,128)(2,1)}), bf16[3,64,2,288]{3,2,0,1:T(2,128)(2,1)S(1)}, u32[]{:S(2)}, u32[]{:S(2)}) async-start(bf16[3,64,2,288]{3,2,0,1:T(2,128)(2,1)} %copy.100), calls=%async_computation.3 | async-start | bytes 589824 | tf_op jit(solution)/shard_map/all_to_all | solution.py:104
  220.2 282.9 %all-reduce.5.cloned.1.call-start = ((), (), s32[]{:S(2)}) async-start(), calls=%async_computation.5 | async-start | bytes 3538944
  222.4 350.0 %all-reduce.7.cloned.1.call-start = ((), (), s32[]{:S(2)}) async-start(), calls=%async_computation.6 | async-start | bytes 2359296 | tf_op jit(solution)/shard_map/psum | solution.py:72
Sparse Core Ops, SparseCore 0:
  11.5 142.6 all-gather.2
  224.5 278.5 all-reduce.4
  506.1 66.2 all-reduce.6
where the time goes:
time: 583 us
  waiting for transfers between devices  416 us (71%)
  blocking collectives  87 us (15%)
  starting transfers between devices  28.3 us (5%)
  between operations  14.9 us (3%)
  local copies, waits for them, and re-layouts  14.8 us (3%)
  matrix products  14.7 us (3%)
  other arithmetic  6.4 us (1%)
    unnamed x4, waiting for transfers between devices  256 us
    all_gather x1, blocking collectives, per_device(): lax.all_gather(proj_weight, 'frame', axis=1, tiled=True)  87 us
    psum x1, waiting for transfers between devices, per_device(): branch = lax.psum(partial_branch, 'head')  67.9 us
    all_gather x1, waiting for transfers between devices, per_device(): lax.all_gather(qkv_weight, 'frame', axis=1, tiled=True)  45.9 us
    all_to_all x1, waiting for transfers between devices, per_device(): lax.all_to_all(stacked, 'frame', split_axis=2, concat_axis=1, tiled=True)  18.7 us
    all_to_all x1, waiting for transfers between devices, per_device(): lax.all_to_all(d_stack, 'frame', split_axis=1, concat_axis=2, tiled=True)  14.7 us
    all_to_all x1, waiting for transfers between devices, per_device(): lax.all_to_all(attended_s, 'frame', split_axis=0, concat_axis=1, tiled=True)  12.8 us
  transfers between devices with their start and end apart: 7, of which 6 were waited for; matrix products, arithmetic and copies ran while one was open for 4% of the time, Pallas kernels for 0%

commit v1 on v0

v1 whole, which is shorter than its diff:
```python
import jax
import jax.numpy as jnp
import numpy as np
from jax import lax
from jax.experimental import pallas as pl
from jax.experimental.pallas import tpu as pltpu
from jax.sharding import PartitionSpec as P

MESH = pl.DeviceIdType.MESH
BF = jnp.bfloat16
F32 = jnp.float32
NZ, NX, NY = 16, 4, 4
HD = 72
FPAD = 320
WCOLS = 576

S_WX = 0
S_RR = S_WX + 3
S_RL = S_RR + 8
S_X1 = S_RL + 7
S_Z1 = S_X1 + 3
S_AY = S_Z1 + 15
S_AC = S_AY + 3
S_B = S_AC + 4
S_H = S_B + 4
S_Z2 = S_H + 4
S_X2 = S_Z2 + 15
S_OY = S_X2 + 3
S_OC = S_OY + 1
S_PX = S_OC + 2
S_PZ = S_PX + 3
S_PY = S_PZ + 15
N_SEM = S_PY + 1


def one_hot(shape, pairs):
    m = np.zeros(shape, np.float32)
    for r, c in pairs:
        m[r, c] = 1.0
    return m.astype(jnp.bfloat16)


def selections():
    r2, r4, r16, r18, r72 = range(2), range(4), range(16), range(18), range(72)
    return [
        one_hot((80, 128), [(x * 18 + j, x * 32 + j) for x in r4 for j in r18]),
        one_hot((WCOLS, 1024), [(g * 72 + j, g * 128 + j) for g in range(8) for j in r72]),
        one_hot((256, 256), [(z * 16 + a * 8 + x * 2 + i, x * 64 + z * 4 + a * 2 + i) for z in r16 for x in r4 for a in r2 for i in r2]),
        one_hot((256, 256), [(a * 128 + z * 8 + x * 2 + i, z * 16 + a * 8 + x * 2 + i) for z in r16 for x in r4 for a in r2 for i in r2]),
        one_hot((256, 256), [(x * 64 + a * 32 + z * 2 + i, z * 16 + a * 8 + x * 2 + i) for z in r16 for x in r4 for a in r2 for i in r2]),
        one_hot((256, 256), [(a * 128 + z * 8 + x * 2 + i, x * 64 + a * 32 + z * 2 + i) for z in r16 for x in r4 for a in r2 for i in r2]),
        one_hot((FPAD, 288), [(g * 80 + j, g * 72 + j) for g in r4 for j in r72]),
        one_hot((FPAD, FPAD), [(z * 80 + x * 18 + j, x * 80 + z * 18 + j) for z in r4 for x in r4 for j in r18]),
        one_hot((128, 80), [(z * 32 + j, z * 18 + j) for z in r4 for j in r18]),
        one_hot((256, 288), [(h * 128 + j, h * 72 + j) for h in r2 for j in r72]),
        one_hot((256, 288), [(h * 128 + j, 144 + h * 72 + j) for h in r2 for j in r72]),
    ]


def dot(a, b):
    return jnp.dot(a, b, preferred_element_type=F32)


def dot_nt(a, b):
    return lax.dot_general(a, b, (((1,), (1,)), ((), ())), preferred_element_type=F32)


def dot_tn(a, b):
    return lax.dot_general(a, b, (((0,), (0,)), ((), ())), preferred_element_type=F32)


def mod(a, n):
    return lax.rem(a + n, n)


def kernel(
    w_in, rows_in, qg_ref, kg_ref, sel80, place, p_x1, p_z1, p_z2, p_x2, unpad, p_pg, p_pz, p_h0, p_h1,
    out_ref, pg_ref,
    xb, g, wp, r1, z1, r2, a, bp, bq, bt, bu, hp, hq, ht, hu, zb, r3, xs, r4, oa, px, pxr, pz, pzr, pgs,
    ss, rs,
):
    f, hd, dp = lax.axis_index("frame"), lax.axis_index("head"), lax.axis_index("dp")
    z, x = f // NX, lax.rem(f, NX)
    core, y = lax.rem(hd, 2), (hd // 2) * 2 + dp

    def at_x(d):
        return (z * NX + mod(x + d, NX), hd, dp)

    def at_z(d):
        return (mod(z + d, NZ) * NX + x, hd, dp)

    def at_y(d):
        yy = mod(y + d, NY)
        return (f, (yy // 2) * 2 + core, lax.rem(yy, 2))

    across = (f, hd + 1 - 2 * core, dp)

    def copy(src, dst, i, dev):
        return pltpu.make_async_remote_copy(
            src_ref=src, dst_ref=dst, send_sem=ss.at[i], recv_sem=rs.at[i], device_id=dev, device_id_type=MESH
        )

    sends = []

    def send(*args):
        c = copy(*args)
        c.start()
        sends.append(c)

    def landed(ref, i):
        copy(ref, ref, i, across).wait_recv()

    barrier = pltpu.get_barrier_semaphore()

    def greet(dev):
        pl.semaphore_signal(barrier, inc=1, device_id=dev, device_id_type=MESH)

    with jax.named_scope("greet"):
        for d in range(1, NX):
            greet(at_x(d))
        for d in range(1, NY):
            greet(at_y(d))
        greet(across)

        def greet_z(d, c):
            greet(at_z(d))
            return c

        lax.fori_loop(1, NZ, greet_z, 0)
        pl.semaphore_wait(barrier, 22)

    def z_send(src, dst, base):
        def step(d, c):
            copy(src.at[mod(z + d, NZ)], dst.at[z], base + d - 1, at_z(d)).start()
            return c

        lax.fori_loop(1, NZ, step, 0)

    def z_landed(dst, base):
        def step(d, c):
            landed(dst.at[mod(z - d, NZ)], base + d - 1)
            return c

        lax.fori_loop(1, NZ, step, 0)

    def z_sent(src, dst, base):
        def step(d, c):
            copy(src.at[mod(z + d, NZ)], dst.at[z], base + d - 1, at_z(d)).wait_send()
            return c

        lax.fori_loop(1, NZ, step, 0)

    with jax.named_scope("along_x"):
        for d in range(1, NX):
            send(w_in, xb.at[x], S_WX + d - 1, at_x(d))
        for d in range(1, NX):
            send(rows_in.at[mod(x + d, NX)], r1.at[x], S_X1 + d - 1, at_x(d))
        xb[x] = w_in[...]
        r1[x] = rows_in[x]
        for d in range(1, NX):
            landed(xb.at[mod(x - d, NX)], S_WX + d - 1)
        g[z] = dot(sel80[...], xb[...].reshape(128, WCOLS)).astype(BF)

    def put(c):
        wp[c] = dot(g[c], place[...]).astype(BF)

    def right(s):
        c = mod(z - s + 1, NZ)
        return copy(g.at[c], g.at[c], S_RR + s - 1, at_z(1))

    def left(s):
        c = mod(z + s - 1, NZ)
        return copy(g.at[c], g.at[c], S_RL + s - 1, at_z(-1))

    def ring(lo, hi):
        def step(s, c):
            right(s).start()
            left(s).start()
            put(mod(z - s + 1, NZ))
            put(mod(z + s - 1, NZ))
            landed(g.at[mod(z - s, NZ)], S_RR + s - 1)
            landed(g.at[mod(z + s, NZ)], S_RL + s - 1)
            return c

        lax.fori_loop(lo, hi, step, 0)

    with jax.named_scope("ring_a"):
        ring(1, 2)
    with jax.named_scope("rows_x"):
        for d in range(1, NX):
            landed(r1.at[mod(x - d, NX)], S_X1 + d - 1)
        z1[...] = dot(p_x1[...], r1[...].reshape(256, FPAD)).astype(BF).reshape(NZ, 16, FPAD)
        z_send(z1, r2, S_Z1)
        r2[z] = z1[z]
    with jax.named_scope("ring_b"):
        ring(2, 4)
    with jax.named_scope("rows_z"):
        z_landed(r2, S_Z1)
        a[core, y] = dot(p_z1[...], r2[...].reshape(256, FPAD)).astype(BF)
        for d in range(1, NY):
            send(a.at[core, y], a.at[core, y], S_AY + d - 1, at_y(d))
        send(a.at[core, y], a.at[core, y], S_AC, across)
    with jax.named_scope("ring_c"):
        ring(4, 7)
    with jax.named_scope("rows_y"):
        for d in range(1, NY):
            slot = a.at[core, mod(y - d, NY)]
            landed(slot, S_AY + d - 1)
            send(slot, slot, S_AC + d, across)
    with jax.named_scope("ring_d"):
        ring(7, 8)
        right(8).start()
        put(mod(z - 7, NZ))
        put(mod(z + 7, NZ))
        for d in range(NY):
            landed(a.at[1 - core, mod(y - d, NY)], S_AC + d)

    def rows_of(q, arr):
        lo = arr * 128
        return jnp.concatenate([a[q % 2, (q // 2) * 2 + p, lo : lo + 128, :] for p in range(2)], axis=0)

    db_q = [rows_of(q, 1) for q in range(4)]
    with jax.named_scope("ring_e"):
        landed(g.at[mod(z - 8, NZ)], S_RR + 7)
        put(mod(z - 8, NZ))

    with jax.named_scope("project"):

        def w_of(q, lo, hi):
            return wp[4 * q : 4 * q + 4, :, lo:hi].reshape(FPAD, hi - lo)

        raw = dot(rows_of(0, 0), w_of(0, 0, 768))
        d_att = dot(db_q[0], w_of(0, 768, 1024))
        for q in range(1, 4):
            raw += dot(rows_of(q, 0), w_of(q, 0, 768))
            d_att += dot(db_q[q], w_of(q, 768, 1024))
        d_att = d_att.astype(BF)

    q_gain, k_gain = qg_ref[...], kg_ref[...]
    factor = 1.0 / np.sqrt(np.float32(HD))
    row_i = lax.broadcasted_iota(jnp.int32, (128, 128), 0) % 2
    col_i = lax.broadcasted_iota(jnp.int32, (128, 128), 1) % 2
    same = row_i == col_i

    def norm(v, gain):
        root = lax.rsqrt(jnp.sum(v * v, axis=-1, keepdims=True) * (1.0 / HD) + 1e-06)
        return (v * root * gain).astype(BF), root

    with jax.named_scope("attend"):
        state = []
        att = []
        for p in range(2):
            for h in range(2):
                rows = slice(128 * p, 128 * p + 128)
                rq, rk = raw[rows, 128 * h : 128 * h + 128], raw[rows, 256 + 128 * h : 384 + 128 * h]
                v = raw[rows, 512 + 128 * h : 640 + 128 * h].astype(BF)
                qn, root_q = norm(rq, q_gain)
                kn, root_k = norm(rk, k_gain)
                s = jnp.where(same, dot_nt(qn, kn) * factor, -1e30)
                e = jnp.exp(s - jnp.max(s, axis=-1, keepdims=True))
                pr = e / jnp.sum(e, axis=-1, keepdims=True)
                pb = pr.astype(BF)
                att.append(dot(pb, v).astype(BF))
                state.append((rq, rk, v, qn, kn, root_q, root_k, pr, pb))
        att = jnp.concatenate(
            [jnp.concatenate([att[0], att[1]], axis=1), jnp.concatenate([att[2], att[3]], axis=1)], axis=0
        )

    def spread(q, val, buf):
        for p in range(2):
            buf[q % 2, (q // 2) * 2 + p] = val[128 * p : 128 * p + 128].astype(BF)

    with jax.named_scope("branch"):
        for q in range(4):
            spread(q, dot_nt(att, w_of(q, 768, 1024)), bp)
        send(bp.at[1 - core], bq, S_B, across)

    with jax.named_scope("proj_grad"):
        att_c = jnp.concatenate(
            [dot(att[:128], p_h0[...]).astype(BF), dot(att[128:], p_h1[...]).astype(BF)], axis=0
        )
        for q in range(4):
            dbx = dot(db_q[q], p_pg[...]).astype(BF)
            px[:, 80 * q : 80 * q + 80] = dot_tn(dbx, att_c).astype(BF).reshape(NX, 80, 288)
        for d in range(1, NX):
            to = mod(x + d, NX)
            send(px.at[to], pxr.at[d - 1], S_PX + d - 1, at_x(d))

    with jax.named_scope("attend_back"):
        d_raw = [[], []]
        for p in range(2):
            cols_q, cols_k, cols_v = [], [], []
            for h in range(2):
                rq, rk, v, qn, kn, root_q, root_k, pr, pb = state[2 * p + h]
                da = d_att[128 * p : 128 * p + 128, 128 * h : 128 * h + 128]
                dv = dot_tn(pb, da).astype(BF)
                d_p = dot_nt(da, v)
                ds = (pr * (d_p - jnp.sum(pr * d_p, axis=-1, keepdims=True)) * factor).astype(BF)
                dq = dot(ds, kn).astype(BF)
                dk = dot_tn(ds, qn).astype(BF)

                def norm_back(v_raw, root, gain, d_n):
                    gq = gain * d_n.astype(F32)
                    inner = jnp.sum(v_raw * gq, axis=-1, keepdims=True) * (1.0 / HD)
                    return (root * gq - v_raw * (root * root * root) * inner).astype(BF)

                cols_q.append(norm_back(rq, root_q, q_gain, dq))
                cols_k.append(norm_back(rk, root_k, k_gain, dk))
                cols_v.append(dv)
            d_raw[p] = jnp.concatenate(cols_q + cols_k + cols_v, axis=1)
        d_raw = jnp.concatenate(d_raw, axis=0)
        for q in range(4):
            spread(q, dot_nt(d_raw, w_of(q, 0, 768)), hp)
        send(hp.at[1 - core], hq, S_H, across)

    def to_y(own, got, total, far, base):
        landed(got, base)
        total[...] = (own[core].astype(F32) + got[...].astype(F32)).astype(BF)
        for d in range(1, NY):
            send(total.at[mod(y + d, NY)], far.at[d - 1], base + d, at_y(d))

    def y_sum(total, far, base):
        for d in range(1, NY):
            landed(far.at[d - 1], base + d)
        s = total[y].astype(F32)
        for d in range(1, NY):
            s += far[d - 1].astype(F32)
        return s

    with jax.named_scope("branch_y"):
        to_y(bp, bq, bt, bu, S_B)
    with jax.named_scope("hidden_y"):
        to_y(hp, hq, ht, hu, S_H)
    with jax.named_scope("grad_x"):
        for d in range(1, NX):
            landed(pxr.at[d - 1], S_PX + d - 1)
        s = px[x].astype(F32)
        for d in range(1, NX):
            s += pxr[d - 1].astype(F32)
        s = s.astype(BF)
        for q in range(4):
            pz[4 * q : 4 * q + 4] = dot(p_pz[...], s[80 * q : 80 * q + 80]).astype(BF).reshape(4, 32, 288)
        z_send(pz, pzr, S_PZ)
        pzr[z] = pz[z]
    with jax.named_scope("back_z"):
        branch = y_sum(bt, bu, S_B)
        hidden = y_sum(ht, hu, S_H)
        both = jnp.concatenate([branch.reshape(NZ, 8, FPAD), hidden.reshape(NZ, 8, FPAD)], axis=1)
        zb[...] = both.astype(BF)
        z_send(zb, r3, S_Z2)
        r3[z] = zb[z]
        z_landed(r3, S_Z2)
    with jax.named_scope("back_x"):
        xs[...] = dot(p_z2[...], r3[...].reshape(256, FPAD)).astype(BF).reshape(NX, 64, FPAD)
        for d in range(1, NX):
            send(xs.at[mod(x + d, NX)], r4.at[x], S_X2 + d - 1, at_x(d))
        r4[x] = xs[x]
        for d in range(1, NX):
            landed(r4.at[mod(x - d, NX)], S_X2 + d - 1)
        own = dot(p_x2[...], r4[...].reshape(256, FPAD)).astype(BF)
        oa[hd] = dot(own, unpad[...]).astype(BF)
    with jax.named_scope("back_head"):
        far_hd = mod(hd + 2, 4)
        send(oa.at[hd], oa.at[hd], S_OY, at_y(2))
        send(oa.at[hd], oa.at[hd], S_OC, across)
    with jax.named_scope("grad_z"):
        z_landed(pzr, S_PZ)
        s = pzr[0].astype(F32)
        for k in range(1, NZ):
            s += pzr[k].astype(F32)
        pgs[dp] = s
        send(pgs.at[dp], pgs.at[dp], S_PY, at_y(1 - 2 * dp))
    with jax.named_scope("back_core"):
        landed(oa.at[far_hd], S_OY)
        send(oa.at[far_hd], oa.at[far_hd], S_OC + 1, across)
        landed(oa.at[hd + 1 - 2 * core], S_OC)
        landed(oa.at[mod(hd + 3 - 2 * core, 4)], S_OC + 1)
        out_ref[...] = oa[...]
        landed(pgs.at[1 - dp], S_PY)
        pg_ref[...] = pgs[...]

    with jax.named_scope("sent"):
        for c in sends:
            c.wait_send()

        def ring_sent(s, c):
            right(s).wait_send()
            left(s).wait_send()
            return c

        lax.fori_loop(1, 8, ring_sent, 0)
        right(8).wait_send()
        z_sent(z1, r2, S_Z1)
        z_sent(zb, r3, S_Z2)
        z_sent(pz, pzr, S_PZ)


def per_device(inputs, modulation, qkv_weight, proj_weight, q_gain, k_gain, cotangent):
    _, spatial_n, width = inputs.shape
    hd, dp = lax.axis_index("head"), lax.axis_index("dp")
    inputs_f = inputs[0].astype(F32)
    shift_vec, scale_vec, gate_vec = (modulation[0], modulation[1], modulation[2])
    center = jnp.mean(inputs_f, axis=1, keepdims=True)
    centered = inputs_f - center
    rstd_col = 1.0 / jnp.sqrt(jnp.mean(centered * centered, axis=1, keepdims=True) + 1e-06)
    normed = centered * rstd_col
    hidden_in = (normed * (1.0 + scale_vec) + shift_vec).astype(BF)
    d_out = cotangent[0].astype(F32)
    d_branch = (gate_vec * d_out).astype(BF)

    both = jnp.stack([hidden_in, d_branch])
    both = lax.dynamic_slice_in_dim(both, hd * 288, 288, axis=2)
    both = both.reshape(2, NZ, NX, 2, 4, HD).transpose(2, 1, 0, 3, 4, 5)
    both = jnp.pad(both, [(0, 0)] * 5 + [(0, 8)]).reshape(NX, 64, FPAD)

    w_half = lax.dynamic_slice_in_dim(qkv_weight, dp * 144, 144, axis=2)
    w_half = w_half.transpose(1, 0, 2).reshape(18, 432)
    p_half = lax.dynamic_slice_in_dim(proj_weight, dp * 144, 144, axis=0).T
    w_in = jnp.pad(jnp.concatenate([w_half, p_half], axis=1), [(0, 14), (0, 0)])

    gains = [jnp.pad(v, (0, 56)).reshape(1, 128) for v in (q_gain, k_gain)]
    consts = [jnp.asarray(m) for m in selections()]

    def vm(*shape, dtype=BF):
        return pltpu.VMEM(shape, dtype)

    out, pg = pl.pallas_call(
        kernel,
        out_shape=(
            jax.ShapeDtypeStruct((4, 256, 288), BF),
            jax.ShapeDtypeStruct((2, 32, 288), F32),
        ),
        in_specs=[pl.BlockSpec(memory_space=pltpu.VMEM)] * (4 + len(consts)),
        out_specs=[pl.BlockSpec(memory_space=pltpu.VMEM)] * 2,
        scratch_shapes=[
            vm(NX, 32, WCOLS),
            vm(NZ, 80, WCOLS),
            vm(NZ, 80, 1024),
            vm(NX, 64, FPAD),
            vm(NZ, 16, FPAD),
            vm(NZ, 16, FPAD),
            vm(2, NY, 256, FPAD),
            vm(2, NY, 128, FPAD),
            vm(NY, 128, FPAD),
            vm(NY, 128, FPAD),
            vm(3, 128, FPAD),
            vm(2, NY, 128, FPAD),
            vm(NY, 128, FPAD),
            vm(NY, 128, FPAD),
            vm(3, 128, FPAD),
            vm(NZ, 16, FPAD),
            vm(NZ, 16, FPAD),
            vm(NX, 64, FPAD),
            vm(NX, 64, FPAD),
            vm(4, 256, 288),
            vm(NX, 320, 288),
            vm(3, 320, 288),
            vm(NZ, 32, 288),
            vm(NZ, 32, 288),
            vm(2, 32, 288, dtype=F32),
            pltpu.SemaphoreType.DMA((N_SEM,)),
            pltpu.SemaphoreType.DMA((N_SEM,)),
        ],
        compiler_params=pltpu.CompilerParams(
            collective_id=0, has_side_effects=True, vmem_limit_bytes=48 * 1024 * 1024
        ),
    )(w_in, both, *gains, *consts)

    out = out.reshape(4, 2, spatial_n, 288).transpose(1, 2, 0, 3).reshape(2, spatial_n, width)
    branch, d_hidden = out[0].astype(F32), out[1].astype(F32)
    output = (inputs_f + gate_vec * branch).astype(BF)
    d_normed = d_hidden * (1.0 + scale_vec)
    d_in = rstd_col * (
        d_normed
        - jnp.mean(d_normed, axis=1, keepdims=True)
        - normed * jnp.mean(d_normed * normed, axis=1, keepdims=True)
    )
    input_grad = (d_out + d_in).astype(BF)
    pg = lax.dynamic_slice(pg, (0, 0, dp * 144), (2, 18, 144))
    proj_grad = pg.transpose(0, 2, 1).reshape(288, 18)
    return output[None], input_grad[None], proj_grad


def solution(mesh):
    return jax.shard_map(
        per_device,
        mesh=mesh,
        in_specs=(
            P(("dp", "frame"), None, None),
            P("dp", None),
            P(None, "frame", "head"),
            P("head", "frame"),
            P(),
            P(),
            P(("dp", "frame"), None, None),
        ),
        out_specs=(
            P(("dp", "frame"), None, None),
            P(("dp", "frame"), None, None),
            P(("dp", "head"), "frame"),
        ),
        check_vma=False,
    )
```

time: 583 us -> 129 us (0.22)
  waiting for transfers between devices: 416 us -> 0 us
  Pallas kernels: 0 us -> 118 us
  blocking collectives: 87 us -> 0 us
  starting transfers between devices: 28.3 us -> 0 us
  matrix products: 14.7 us -> 0 us
  between operations: 14.9 us -> 1.04 us
  local copies, waits for them, and re-layouts: 14.8 us -> 7.29 us
    unnamed x4 -> x0, waiting for transfers between devices: 256 us -> none
    pallas_call x0 -> x1, Pallas kernels: none -> 118 us  [per_device(): pl.pallas_call(kernel, out_shape=(jax.ShapeDtypeStruct((4, 256, 288), BF)...]
    all_gather x1 -> x0, blocking collectives: 87 us -> none  [per_device(): lax.all_gather(proj_weight, 'frame', axis=1, tiled=True)]
    psum x1 -> x0, waiting for transfers between devices: 67.9 us -> none  [per_device(): branch = lax.psum(partial_branch, 'head')]
    all_to_all x4 -> x0, waiting for transfers between devices: 46.2 us -> none  [the longest x1 18.7 us: per_device(): lax.all_to_all(stacked, 'frame', split_axis=2, concat_axis=1, tiled=True)]
    all_gather x1 -> x0, waiting for transfers between devices: 45.9 us -> none  [per_device(): lax.all_gather(qkv_weight, 'frame', axis=1, tiled=True)]
    all_to_all x4 -> x0, starting transfers between devices: 28.2 us -> none  [the longest x1 10 us: per_device(): lax.all_to_all(stacked, 'frame', split_axis=2, concat_axis=1, tiled=True)]
    dot_general x10 -> x0, matrix products: 13.8 us -> none  [the longest x1 3.77 us: per_device(): jnp.einsum('wre,wne->rn', d_raw, lax.all_gather(qkv_weight, 'frame', axis...]
  transfers between devices with their start and end apart: 7 -> 0, of which waited for: 6 -> 0; matrix products, arithmetic and copies ran while one was open for 4% -> 0% of each run, Pallas kernels for 0% -> 0%
where the time goes in v1:
time: 129 us; the launch traced here: 128 us
  Pallas kernels  118 us (91%)
  local copies, waits for them, and re-layouts  7.29 us (6%)
  other arithmetic  1.7 us (1%)
    pallas_call x1, Pallas kernels, per_device(): pl.pallas_call(kernel, out_shape=(jax.ShapeDtypeStruct((4, 256, 288), BF)...  118 us
    unnamed x61, local copies, waits for them, and re-layouts  5.02 us

profile of v1, /device:TPU:1, one launch (start us, length us, event | category | flops | bytes accessed | tf_op | source)
XLA Modules:
  0.0 128.4 jit_solution(6375791470601605912)
XLA Ops:
  0.7 1.2 copy.25
  1.9 0.2 convert_reduce_fusion
  2.1 0.2 fusion.8
  2.3 0.2 copy.27
  2.6 0.5 fusion
  3.2 0.1 copy-done.15
  3.3 0.2 copy.28
  3.6 0.2 reshape.259
  3.8 0.1 copy.34
  3.9 0.1 pad.16.clone
  4.0 0.2 reshape.260.rows_in
  4.2 0.1 dynamic-slice_bitcast_fusion.1
  4.3 0.1 reshape.258
  4.7 0.1 copy-done.1
  5.1 118.3 %shard_map.193 = (bf16[4,256,288]{2,1,0:T(8,128)(2,1)S(1)}, f32[2,32,288]{2,1,0:T(8,128)S(1)}) custom-call(bf16[32,576]{1,0:T(8,128)(2,1)S(1)} %fusion.12.w_in, bf16[4,64,320]{2,1,0:T(8,128)(2,1)S(1)} %reshape.260.rows_in, f32[1,128]{1,0:T(1,128)S(1)} %get-tuple-element.20.qg_ref, f32[1,128]{1,0:T(1,128)S(1)} %get-tuple-element.19.kg_ref, ...), custom_call_target="tpu_custom_call" | custom-call | tf_op jit(solution)/shard_map/pallas_call | solution.py:427
  123.4 0.6 copy-done.10
  124.1 0.4 copy.30
  124.5 0.3 copy-done.19
  124.8 0.2 copy-done.14
  125.0 0.2 multiply_reduce_fusion.1
  125.3 0.4 fusion.1
  125.8 0.9 copy.32
  126.7 0.9 copy.33
  127.7 0.7 reshape.264
  (65 shorter events, 0.9 us)
Async XLA Ops:
  0.6 3.6 %copy-start = (bf16[3,18,288]{2,1,0:T(8,128)(2,1)S(1)}, bf16[3,18,288]{2,1,0:T(8,128)(2,1)}, u32[]{:S(2)}) copy-start(bf16[3,18,288]{2,1,0:T(8,128)(2,1)} %param.20) | copy-start | bytes 93316
  0.6 1.6 %copy-start.22 = (f32[3,1152]{1,0:T(4,128)S(1)}, f32[3,1152]{1,0:T(4,128)}, u32[]{:S(2)}) copy-start(f32[3,1152]{1,0:T(4,128)} %param.19) | copy-start | bytes 41476
  0.7 1.7 %copy-start.17 = (bf16[1,128,1152]{2,1,0:T(8,128)(2,1)S(1)}, bf16[1,128,1152]{2,1,0:T(8,128)(2,1)}, u32[]{:S(2)}) copy-start(bf16[1,128,1152]{2,1,0:T(8,128)(2,1)} %param.24) | copy-start | bytes 884740
  1.9 1.2 copy-start.13
  2.2 0.9 copy-start.24
  2.3 0.8 copy-start.18
  3.3 1.2 copy-start.23
  3.3 1.4 %copy-start.7 = (bf16[256,256]{1,0:T(8,128)(2,1)S(1)}, bf16[256,256]{1,0:T(8,128)(2,1)}, u32[]{:S(2)}) copy-start(bf16[256,256]{1,0:T(8,128)(2,1)} %constant.55.clone.p_z1) | copy-start | bytes 393220
  3.3 1.4 %copy-start.8 = (bf16[256,256]{1,0:T(8,128)(2,1)S(1)}, bf16[256,256]{1,0:T(8,128)(2,1)}, u32[]{:S(2)}) copy-start(bf16[256,256]{1,0:T(8,128)(2,1)} %constant.56.clone.p_z2) | copy-start | bytes 393220
  3.5 1.2 copy-start.26
  3.5 1.2 copy-start.27
  3.5 1.3 %copy-start.1 = (bf16[576,1024]{1,0:T(8,128)(2,1)S(1)}, bf16[576,1024]{1,0:T(8,128)(2,1)}, u32[]{:S(2)}) copy-start(bf16[576,1024]{1,0:T(8,128)(2,1)} %constant.53.clone.place) | copy-start | bytes 3538948
  3.5 1.3 %copy-start.2 = (bf16[256,256]{1,0:T(8,128)(2,1)S(1)}, bf16[256,256]{1,0:T(8,128)(2,1)}, u32[]{:S(2)}) copy-start(bf16[256,256]{1,0:T(8,128)(2,1)} %constant.54.clone.p_x1.p_x2) | copy-start | bytes 393220
  3.5 1.4 %copy-start.3 = (bf16[320,288]{1,0:T(8,128)(2,1)S(1)}, bf16[320,288]{1,0:T(8,128)(2,1)}, u32[]{:S(2)}) copy-start(bf16[320,288]{1,0:T(8,128)(2,1)} %constant.57.clone.unpad) | copy-start | bytes 552964
  3.5 1.4 %copy-start.4 = (bf16[320,320]{1,0:T(8,128)(2,1)S(1)}, bf16[320,320]{1,0:T(8,128)(2,1)}, u32[]{:S(2)}) copy-start(bf16[320,320]{1,0:T(8,128)(2,1)} %constant.58.clone.p_pg) | copy-start | bytes 614404
  3.5 1.5 %copy-start.5 = (bf16[256,288]{1,0:T(8,128)(2,1)S(1)}, bf16[256,288]{1,0:T(8,128)(2,1)}, u32[]{:S(2)}) copy-start(bf16[256,288]{1,0:T(8,128)(2,1)} %constant.60.clone.p_h0) | copy-start | bytes 442372
  3.6 1.5 %copy-start.6 = (bf16[256,288]{1,0:T(8,128)(2,1)S(1)}, bf16[256,288]{1,0:T(8,128)(2,1)}, u32[]{:S(2)}) copy-start(bf16[256,288]{1,0:T(8,128)(2,1)} %constant.61.clone.p_h1) | copy-start | bytes 442372
  3.6 1.5 %copy-start.9 = (bf16[128,80]{1,0:T(8,128)(2,1)S(1)}, bf16[128,80]{1,0:T(8,128)(2,1)}, u32[]{:S(2)}) copy-start(bf16[128,80]{1,0:T(8,128)(2,1)} %constant.59.clone.p_pz) | copy-start | bytes 61444
  3.6 1.5 %copy-start.12 = (bf16[80,128]{1,0:T(8,128)(2,1)S(1)}, bf16[80,128]{1,0:T(8,128)(2,1)}, u32[]{:S(2)}) copy-start(bf16[80,128]{1,0:T(8,128)(2,1)} %constant.52.clone.sel80) | copy-start | bytes 61444
  124.0 1.0 copy-start.14
  124.0 1.0 copy-start.25
  124.1 1.2 copy-start.16
  124.1 1.2 copy-start.21
  125.3 2.2 %copy-start.11 = (f32[2,32,288]{2,1,0:T(8,128)S(1)}, f32[2,32,288]{2,1,0:T(8,128)}, u32[]{:S(2)}) copy-start(f32[2,32,288]{2,1,0:T(8,128)} %copy-done.10) | copy-start | bytes 221188
  (4 other events, 2.9 us)

commit v2 on v1

v2 whole, which is shorter than its diff:
```python
import jax
import jax.numpy as jnp
import numpy as np
from jax import lax
from jax.experimental import pallas as pl
from jax.experimental.pallas import tpu as pltpu
from jax.sharding import PartitionSpec as P

MESH = pl.DeviceIdType.MESH
BF = jnp.bfloat16
F32 = jnp.float32
NZ, NX, NY = 16, 4, 4
HD = 72
QF = 288
QKV, WCOLS = 432, 576

S_X1 = 0
S_WZ = S_X1 + 3
S_Z1 = S_WZ + 15
S_WX = S_Z1 + 15
S_AY = S_WX + 3
S_AC = S_AY + 3
S_B = S_AC + 4
S_H = S_B + 4
S_Z2 = S_H + 4
S_X2 = S_Z2 + 15
S_XF = S_X2 + 3
S_OC = S_XF + 4
S_PX = S_OC + 2
S_PZ = S_PX + 3
S_PY = S_PZ + 15
N_SEM = S_PY + 1


def one_hot(shape, pairs):
    m = np.zeros(shape, np.float32)
    for r, c in pairs:
        m[r, c] = 1.0
    return m.astype(jnp.bfloat16)


def selections():
    r2, r4, r16 = range(2), range(4), range(16)
    rows = [(a, z, x, i) for a in r2 for z in r16 for x in r4 for i in r2]
    return [
        one_hot((256, 256), [(x * 64 + z * 4 + a * 2 + i, a * 128 + z * 8 + x * 2 + i) for a, z, x, i in rows]),
        one_hot((256, 256), [(z * 16 + a * 8 + x * 2 + i, x * 64 + z * 4 + a * 2 + i) for a, z, x, i in rows]),
        one_hot((256, 256), [(a * 128 + z * 8 + x * 2 + i, z * 16 + a * 8 + x * 2 + i) for a, z, x, i in rows]),
        one_hot((256, 256), [(x * 64 + a * 32 + z * 2 + i, z * 16 + a * 8 + x * 2 + i) for a, z, x, i in rows]),
        one_hot((256, 256), [(a * 128 + z * 8 + x * 2 + i, x * 64 + a * 32 + z * 2 + i) for a, z, x, i in rows]),
        one_hot((72, WCOLS), [(j, g * 72 + j) for g in range(8) for j in range(72)]),
        one_hot((32, 256), [(r, 8 * r + k) for r in range(32) for k in range(8)]),
        one_hot((256, 32), [(z * 16 + o * 4 + k, z * 2 + o) for z in r16 for o in r2 for k in r4]),
    ]


def dot(a, b):
    return jnp.dot(a, b, preferred_element_type=F32)


def dot_nt(a, b):
    return lax.dot_general(a, b, (((1,), (1,)), ((), ())), preferred_element_type=F32)


def dot_tn(a, b):
    return lax.dot_general(a, b, (((0,), (0,)), ((), ())), preferred_element_type=F32)


def mod(a, n):
    return lax.rem(a + n, n)


def kernel(
    w_in, in_ref, cot_ref, mod_ref, qg_ref, kg_ref, p_x0, p_x1, p_z1, p_z2, p_x2, repeat, sum8, widen,
    out_ref, ig_ref, pg_ref,
    order, rows_in, r1, wz, z1, r2, xw, a, bp, bq, bt, bu, hp, hq, ht, hu, zb, r3, xs, r4, px, pxr, pz, pzr, pgs,
    ss, rs,
):
    f, hd, dp = lax.axis_index("frame"), lax.axis_index("head"), lax.axis_index("dp")
    z, x = f // NX, lax.rem(f, NX)
    core, y = lax.rem(hd, 2), (hd // 2) * 2 + dp
    far_hd = mod(hd + 2, 4)

    def at_x(d):
        return (z * NX + mod(x + d, NX), hd, dp)

    def at_x_far(d):
        return (z * NX + mod(x + d, NX), far_hd, dp)

    def at_z(d):
        return (mod(z + d, NZ) * NX + x, hd, dp)

    def at_y(d):
        yy = mod(y + d, NY)
        return (f, (yy // 2) * 2 + core, lax.rem(yy, 2))

    across = (f, hd + 1 - 2 * core, dp)

    def copy(src, dst, i, dev):
        return pltpu.make_async_remote_copy(
            src_ref=src, dst_ref=dst, send_sem=ss.at[i], recv_sem=rs.at[i], device_id=dev, device_id_type=MESH
        )

    sent = []

    def send(*args):
        c = copy(*args)
        c.start()
        sent.append(c.wait_send)

    def landed(ref, i):
        copy(ref, ref, i, across).wait_recv()

    def z_send(src_of, dst, base):
        def each(d, c):
            copy(src_of(mod(z + d, NZ)), dst.at[z], base + d - 1, at_z(d)).start()
            return c

        lax.fori_loop(1, NZ, each, 0)

        def each_sent(d, c):
            copy(src_of(mod(z + d, NZ)), dst.at[z], base + d - 1, at_z(d)).wait_send()
            return c

        sent.append(lambda: lax.fori_loop(1, NZ, each_sent, 0))

    def z_landed(dst, base):
        def each(d, c):
            landed(dst.at[mod(z - d, NZ)], base + d - 1)
            return c

        lax.fori_loop(1, NZ, each, 0)

    barrier = pltpu.get_barrier_semaphore()

    def greet(dev):
        pl.semaphore_signal(barrier, inc=1, device_id=dev, device_id_type=MESH)

    with jax.named_scope("greet"):

        def greet_z(d, c):
            greet(at_z(d))
            return c

        lax.fori_loop(1, NZ, greet_z, 0)
        for d in range(1, NX):
            greet(at_x(d))
            greet(at_x_far(d))
        for d in range(1, NY):
            greet(at_y(d))
        greet(across)

    def mean(v):
        return jnp.sum(v, axis=1, keepdims=True) * (1.0 / v.shape[1])

    def normalise():
        v = in_ref[...].astype(F32)
        v = v - mean(v)
        root = lax.rsqrt(mean(v * v) + 1e-06)
        return v * root, root

    with jax.named_scope("rows"):
        feature = lax.broadcasted_iota(jnp.int32, (1152, QF), 0)
        col = lax.broadcasted_iota(jnp.int32, (1, QF), 1)
        last = col - 256
        from_col = jnp.where(col < 256, (col // 16) * 72 + col % 16, (last // 2) * 72 + 16 + last % 2)
        for q in range(4):
            order[q] = jnp.where(feature == from_col + 18 * q, 1.0, 0.0).astype(BF)
        normed, _ = normalise()
        hidden_in = (normed * (1.0 + mod_ref[1:2]) + mod_ref[0:1]).astype(BF)
        d_branch = (mod_ref[2:3] * cot_ref[...].astype(F32)).astype(BF)
        quarter = dot(jnp.concatenate([hidden_in, d_branch], axis=0), order[hd]).astype(BF)
        rows_in[...] = dot(p_x0[...], quarter).astype(BF).reshape(NX, 64, QF)

    with jax.named_scope("greeted"):
        pl.semaphore_wait(barrier, 25)

    with jax.named_scope("rows_x"):
        for d in range(1, NX):
            send(rows_in.at[mod(x + d, NX)], r1.at[x], S_X1 + d - 1, at_x(d))
        z_send(lambda k: w_in, wz, S_WZ)
        r1[x] = rows_in[x]
        wz[z] = w_in[...]
        for d in range(1, NX):
            landed(r1.at[mod(x - d, NX)], S_X1 + d - 1)
        z1[...] = dot(p_x1[...], r1[...].reshape(256, QF)).astype(BF).reshape(NZ, 16, QF)
        z_send(lambda k: z1.at[k], r2, S_Z1)
        r2[z] = z1[z]

    with jax.named_scope("weights_z"):
        z_landed(wz, S_WZ)
        xw[x, 0:256] = wz[:, :, 0:WCOLS].reshape(256, WCOLS)
        tail = dot(wz[:, :, WCOLS : WCOLS + 72].reshape(256, 72), repeat[...])
        row8 = lax.broadcasted_iota(jnp.int32, (256, WCOLS), 0) % 8
        group = lax.broadcasted_iota(jnp.int32, (1, WCOLS), 1) // 72
        tail = jnp.where(row8 == group, tail, 0.0).astype(BF)
        xw[x, 256:288] = dot(sum8[...], tail).astype(BF)
        for d in (2, 1, 3):
            send(xw.at[x], xw.at[x], S_WX + d - 1, at_x(d))

    with jax.named_scope("rows_z"):
        z_landed(r2, S_Z1)
        a[core, y] = dot(p_z1[...], r2[...].reshape(256, QF)).astype(BF)
        for d in (2, 1, 3):
            send(a.at[core, y], a.at[core, y], S_AY + d - 1, at_y(d))
        send(a.at[core, y], a.at[core, y], S_AC, across)

    with jax.named_scope("rows_y"):
        for d in (1, 3, 2):
            slot = a.at[core, mod(y - d, NY)]
            landed(slot, S_AY + d - 1)
            send(slot, slot, S_AC + d, across)
        for d in range(NY):
            landed(a.at[1 - core, mod(y - d, NY)], S_AC + d)

    def rows_of(q, arr):
        lo = arr * 128
        return jnp.concatenate([a[q % 2, (q // 2) * 2 + p, lo : lo + 128, :] for p in range(2)], axis=0)

    with jax.named_scope("project"):

        def project(q):
            w = xw[q]
            return dot(rows_of(q, 0), w[:, :QKV]), dot(rows_of(q, 1), w[:, QKV:])

        raw, d_att = project(x)
        for d in (1, 3, 2):
            q = mod(x - d, NX)
            landed(xw.at[q], S_WX + d - 1)
            more_raw, more_d = project(q)
            raw, d_att = raw + more_raw, d_att + more_d
        d_att = d_att.astype(BF)

    q_gain, k_gain = qg_ref[...], kg_ref[...]
    factor = 1.0 / np.sqrt(np.float32(HD))
    row_i = lax.broadcasted_iota(jnp.int32, (128, 128), 0) % 2
    col_i = lax.broadcasted_iota(jnp.int32, (128, 128), 1) % 2
    same = row_i == col_i

    def norm(v, gain):
        root = lax.rsqrt(jnp.sum(v * v, axis=-1, keepdims=True) * (1.0 / HD) + 1e-06)
        return (v * root * gain).astype(BF), root

    def part_cols(v, p, k):
        return v[128 * p : 128 * p + 128, HD * k : HD * k + HD]

    with jax.named_scope("attend"):
        state, att = [], [[], []]
        for p in range(2):
            for h in range(2):
                rq, rk, v = (part_cols(raw, p, 2 * w + h) for w in range(3))
                v = v.astype(BF)
                qn, root_q = norm(rq, q_gain)
                kn, root_k = norm(rk, k_gain)
                s = jnp.where(same, dot_nt(qn, kn) * factor, -1e30)
                e = jnp.exp(s - jnp.max(s, axis=-1, keepdims=True))
                pr = e / jnp.sum(e, axis=-1, keepdims=True)
                pb = pr.astype(BF)
                att[p].append(dot(pb, v).astype(BF))
                state.append((rq, rk, v, qn, kn, root_q, root_k, pr, pb))
        att = [jnp.concatenate(half, axis=1) for half in att]

    def spread(q, val, buf):
        for p in range(2):
            buf[q % 2, (q // 2) * 2 + p] = val[128 * p : 128 * p + 128].astype(BF)

    with jax.named_scope("branch"):
        both = jnp.concatenate(att, axis=0)
        for q in range(4):
            spread(q, dot_nt(both, xw[q, :, QKV:]), bp)
        send(bp.at[1 - core], bq, S_B, across)

    with jax.named_scope("attend_back"):
        d_raw = []
        for p in range(2):
            cols_q, cols_k, cols_v = [], [], []
            for h in range(2):
                rq, rk, v, qn, kn, root_q, root_k, pr, pb = state[2 * p + h]
                da = part_cols(d_att, p, h)
                dv = dot_tn(pb, da).astype(BF)
                d_p = dot_nt(da, v)
                ds = (pr * (d_p - jnp.sum(pr * d_p, axis=-1, keepdims=True)) * factor).astype(BF)
                dq = dot(ds, kn).astype(BF)
                dk = dot_tn(ds, qn).astype(BF)

                def norm_back(v_raw, root, gain, d_n):
                    gq = gain * d_n.astype(F32)
                    inner = jnp.sum(v_raw * gq, axis=-1, keepdims=True) * (1.0 / HD)
                    return (root * gq - v_raw * (root * root * root) * inner).astype(BF)

                cols_q.append(norm_back(rq, root_q, q_gain, dq))
                cols_k.append(norm_back(rk, root_k, k_gain, dk))
                cols_v.append(dv)
            d_raw.append(jnp.concatenate(cols_q + cols_k + cols_v, axis=1))
        d_raw = jnp.concatenate(d_raw, axis=0)
        for q in range(4):
            spread(q, dot_nt(d_raw, xw[q, :, :QKV]), hp)
        send(hp.at[1 - core], hq, S_H, across)

    def to_y(own, got, total, far, base):
        landed(got, base)
        total[...] = (own[core].astype(F32) + got[...].astype(F32)).astype(BF)
        for d in (2, 1, 3):
            send(total.at[mod(y + d, NY)], far.at[d - 1], base + d, at_y(d))

    def y_sum(total, far, base):
        for d in range(1, NY):
            landed(far.at[d - 1], base + d)
        s = total[y].astype(F32)
        for d in range(1, NY):
            s += far[d - 1].astype(F32)
        return s

    with jax.named_scope("branch_y"):
        to_y(bp, bq, bt, bu, S_B)
    with jax.named_scope("hidden_y"):
        to_y(hp, hq, ht, hu, S_H)

    with jax.named_scope("proj_grad"):
        none = jnp.zeros((128, 144), BF)
        att_c = jnp.concatenate(
            [jnp.concatenate([att[0], none], axis=1), jnp.concatenate([none, att[1]], axis=1)], axis=0
        )
        for q in range(4):
            px[q] = dot_tn(rows_of(q, 1), att_c).astype(BF)
        for d in (2, 1, 3):
            send(px.at[mod(x + d, NX)], pxr.at[d - 1], S_PX + d - 1, at_x(d))

    with jax.named_scope("back_z"):
        branch = y_sum(bt, bu, S_B)
        hidden = y_sum(ht, hu, S_H)
        pair = jnp.concatenate([branch.reshape(NZ, 8, QF), hidden.reshape(NZ, 8, QF)], axis=1)
        zb[...] = pair.astype(BF)
        z_send(lambda k: zb.at[k], r3, S_Z2)
        r3[z] = zb[z]

    with jax.named_scope("grad_x"):
        for d in range(1, NX):
            landed(pxr.at[d - 1], S_PX + d - 1)
        s = px[x].astype(F32)
        for d in range(1, NX):
            s += pxr[d - 1].astype(F32)
        tail = dot(widen[...], s[256:288].astype(BF))
        row4 = lax.broadcasted_iota(jnp.int32, (256, QF), 0) % 4
        group = lax.broadcasted_iota(jnp.int32, (1, QF), 1) // 72
        tail = jnp.where(row4 == group, tail, 0.0)
        tail = tail[:, 0:72] + tail[:, 72:144] + tail[:, 144:216] + tail[:, 216:288]
        pz[...] = jnp.concatenate([s[0:256], tail], axis=1).astype(BF).reshape(NZ, 16, 360)
        z_send(lambda k: pz.at[k], pzr, S_PZ)
        pzr[z] = pz[z]

    with jax.named_scope("back_x"):
        z_landed(r3, S_Z2)
        xs[...] = dot(p_z2[...], r3[...].reshape(256, QF)).astype(BF).reshape(NX, 64, QF)
        for d in (2, 1, 3):
            to = mod(x + d, NX)
            send(xs.at[to], r4.at[hd, x], S_XF + d, at_x_far(d))
            send(xs.at[to], r4.at[hd, x], S_X2 + d - 1, at_x(d))
        send(xs.at[x], r4.at[hd, x], S_XF, at_y(2))
        r4[hd, x] = xs[x]
        for d in range(1, NX):
            landed(r4.at[hd, mod(x - d, NX)], S_X2 + d - 1)
        send(r4.at[hd], r4.at[hd], S_OC, across)
        for d in range(NX):
            landed(r4.at[far_hd, mod(x - d, NX)], S_XF + d)
        send(r4.at[far_hd], r4.at[far_hd], S_OC + 1, across)

    with jax.named_scope("grad_z"):
        z_landed(pzr, S_PZ)
        s = pzr[0].astype(F32)
        for k in range(1, NZ):
            s += pzr[k].astype(F32)
        pgs[dp] = s
        send(pgs.at[dp], pgs.at[dp], S_PY, at_y(1 - 2 * dp))

    with jax.named_scope("results"):

        def natural(q):
            return dot_nt(dot(p_x2[...], r4[q].reshape(256, QF)).astype(BF), order[q])

        total = natural(hd) + natural(far_hd)
        landed(r4.at[hd + 1 - 2 * core], S_OC)
        total += natural(hd + 1 - 2 * core)
        landed(r4.at[mod(hd + 3 - 2 * core, 4)], S_OC + 1)
        total += natural(mod(hd + 3 - 2 * core, 4))
        out_ref[...] = (in_ref[...].astype(F32) + mod_ref[2:3] * total[0:128]).astype(BF)
        normed, root = normalise()
        d_n = total[128:256] * (1.0 + mod_ref[1:2])
        d_in = root * (d_n - mean(d_n) - normed * mean(d_n * normed))
        ig_ref[...] = (cot_ref[...].astype(F32) + d_in).astype(BF)
        landed(pgs.at[1 - dp], S_PY)
        pg_ref[...] = pgs[...]

    with jax.named_scope("sent"):
        for wait in sent:
            wait()


def per_device(inputs, modulation, qkv_weight, proj_weight, q_gain, k_gain, cotangent):
    dp = lax.axis_index("dp")
    tokens, width = inputs.shape[1:]

    w_half = lax.dynamic_slice_in_dim(qkv_weight, dp * 144, 144, axis=2)
    w_half = w_half.transpose(1, 0, 2).reshape(18, QKV)
    p_half = lax.dynamic_slice_in_dim(proj_weight, dp * 144, 144, axis=0).T
    w_all = jnp.concatenate([w_half, p_half], axis=1)
    w_in = jnp.concatenate([w_all[:16], w_all[16:].reshape(16, HD)], axis=1)

    consts = [jnp.asarray(m) for m in selections()]

    def vm(*shape, dtype=BF):
        return pltpu.VMEM(shape, dtype)

    out, ig, pg = pl.pallas_call(
        kernel,
        out_shape=(
            jax.ShapeDtypeStruct((tokens, width), BF),
            jax.ShapeDtypeStruct((tokens, width), BF),
            jax.ShapeDtypeStruct((2, 16, 360), F32),
        ),
        in_specs=[pl.BlockSpec(memory_space=pltpu.VMEM)] * (6 + len(consts)),
        out_specs=[pl.BlockSpec(memory_space=pltpu.VMEM)] * 3,
        scratch_shapes=[
            vm(4, 1152, QF),
            vm(NX, 64, QF),
            vm(NX, 64, QF),
            vm(NZ, 16, WCOLS + HD),
            vm(NZ, 16, QF),
            vm(NZ, 16, QF),
            vm(NX, QF, WCOLS),
            vm(2, NY, 256, QF),
            vm(2, NY, 128, QF),
            vm(NY, 128, QF),
            vm(NY, 128, QF),
            vm(3, 128, QF),
            vm(2, NY, 128, QF),
            vm(NY, 128, QF),
            vm(NY, 128, QF),
            vm(3, 128, QF),
            vm(NZ, 16, QF),
            vm(NZ, 16, QF),
            vm(NX, 64, QF),
            vm(4, NX, 64, QF),
            vm(NX, QF, QF),
            vm(3, QF, QF),
            vm(NZ, 16, 360),
            vm(NZ, 16, 360),
            vm(2, 16, 360, dtype=F32),
            pltpu.SemaphoreType.DMA((N_SEM,)),
            pltpu.SemaphoreType.DMA((N_SEM,)),
        ],
        compiler_params=pltpu.CompilerParams(
            collective_id=0, has_side_effects=True, vmem_limit_bytes=48 * 1024 * 1024
        ),
    )(w_in, inputs[0], cotangent[0], modulation, q_gain[None], k_gain[None], *consts)

    pg = jnp.concatenate([pg[:, :, :QF], pg[:, :8, QF:].reshape(2, 2, QF)], axis=1)
    pg = lax.dynamic_slice(pg, (0, 0, dp * 144), (2, 18, 144))
    proj_grad = pg.transpose(0, 2, 1).reshape(288, 18)
    return out[None], ig[None], proj_grad


def solution(mesh):
    return jax.shard_map(
        per_device,
        mesh=mesh,
        in_specs=(
            P(("dp", "frame"), None, None),
            P("dp", None),
            P(None, "frame", "head"),
            P("head", "frame"),
            P(),
            P(),
            P(("dp", "frame"), None, None),
        ),
        out_specs=(
            P(("dp", "frame"), None, None),
            P(("dp", "frame"), None, None),
            P(("dp", "head"), "frame"),
        ),
        check_vma=False,
    )
```

time: 129 us -> 112 us (0.87)
  Pallas kernels: 118 us -> 99.8 us
  local copies, waits for them, and re-layouts: 7.29 us -> 10.9 us
  other arithmetic: 1.7 us -> 0.32 us
    pallas_call x1, Pallas kernels: 118 us -> 99.8 us  [per_device(): pl.pallas_call(kernel, out_shape=(jax.ShapeDtypeStruct((tokens, width), B...]
    unnamed x61 -> x28, local copies, waits for them, and re-layouts: 5.02 us -> 8.89 us
where the time goes in v2:
time: 112 us
  Pallas kernels  99.8 us (89%)
  local copies, waits for them, and re-layouts  10.9 us (10%)
    pallas_call x1, Pallas kernels, per_device(): pl.pallas_call(kernel, out_shape=(jax.ShapeDtypeStruct((tokens, width), B...  99.8 us
    unnamed x28, local copies, waits for them, and re-layouts  8.89 us

profile of v2, /device:TPU:1, one launch (start us, length us, event | category | flops | bytes accessed | tf_op | source)
XLA Modules:
  0.0 111.8 jit_solution(3598831926417408804)
XLA Ops:
  0.7 0.8 copy-done
  1.5 0.1 dynamic-slice_bitcast_fusion
  1.6 0.1 reshape.18
  1.7 0.8 dynamic-slice_bitcast_fusion.1
  2.5 0.1 fusion.2
  2.6 0.1 pad_maximum_fusion.1
  2.6 0.1 reshape.19
  2.7 0.1 pad_maximum_fusion.w_in
  2.8 0.6 copy-done.11
  3.5 0.0 copy-done.12
  3.5 1.0 copy-done.2
  4.5 1.0 copy-done.3
  5.4 0.9 copy-done.6
  6.3 0.9 copy-done.7
  7.2 0.8 copy-done.8
  8.0 0.7 copy-done.9
  8.8 0.7 copy-done.10
  9.5 99.8 %shard_map.166 = (bf16[128,1152]{1,0:T(8,128)(2,1)S(1)}, bf16[128,1152]{1,0:T(8,128)(2,1)S(1)}, f32[2,16,360]{2,1,0:T(8,128)S(1)}) custom-call(bf16[16,648]{1,0:T(8,128)(2,1)S(1)} %pad_maximum_fusion.w_in, bf16[128,1152]{1,0:T(8,128)(2,1)S(1)} %bitcast.15, bf16[128,1152]{1,0:T(8,128)(2,1)S(1)} %bitcast.16, f32[3,1152]{1,0:T(4,128)S(1)} %copy-done.9, ...), custom_call_target="tpu_custom_call" | custom-call | tf_op jit(solution)/shard_map/pallas_call | solution.py:414
  109.3 0.1 slice.15
  109.4 0.1 reshape.20
  109.5 0.1 fusion.1
  109.6 0.7 reshape.21
  110.3 0.7 copy.23
  111.0 0.7 copy.24
  (18 shorter events, 0.1 us)
Async XLA Ops:
  0.6 0.8 copy-start
  1.4 1.4 %copy-start.5 = (bf16[256,256]{1,0:T(8,128)(2,1)S(1)}, bf16[256,256]{1,0:T(8,128)(2,1)}, u32[]{:S(2)}) copy-start(bf16[256,256]{1,0:T(8,128)(2,1)} %constant.26.clone.p_z1) | copy-start | bytes 393220
  1.5 1.3 %copy-start.4 = (bf16[256,256]{1,0:T(8,128)(2,1)S(1)}, bf16[256,256]{1,0:T(8,128)(2,1)}, u32[]{:S(2)}) copy-start(bf16[256,256]{1,0:T(8,128)(2,1)} %constant.24.clone.p_x0) | copy-start | bytes 393220
  1.6 1.3 %copy-start.1 = (bf16[256,256]{1,0:T(8,128)(2,1)S(1)}, bf16[256,256]{1,0:T(8,128)(2,1)}, u32[]{:S(2)}) copy-start(bf16[256,256]{1,0:T(8,128)(2,1)} %constant.25.clone.p_x1.p_x2) | copy-start | bytes 393220
  2.8 0.7 copy-start.11
  2.8 0.7 copy-start.12
  3.5 1.0 copy-start.2
  4.4 1.0 copy-start.3
  5.4 0.9 copy-start.6
  6.3 0.9 copy-start.7
  7.2 0.8 copy-start.8
  8.0 0.7 copy-start.9
  8.8 0.7 copy-start.10

commit v3 on v2

--- a/solution.py
+++ b/solution.py
@@ -11,14 +11,15 @@
 F32 = jnp.float32
 NZ, NX, NY = 16, 4, 4
 HD = 72
-QF = 288
+GF = 80
+QF = 4 * GF
 QKV, WCOLS = 432, 576
 
-S_X1 = 0
-S_WZ = S_X1 + 3
-S_Z1 = S_WZ + 15
-S_WX = S_Z1 + 15
-S_AY = S_WX + 3
+S_Z1 = 0
+S_X1 = S_Z1 + 15
+S_W4 = S_X1 + 3
+S_WX = S_W4 + 3
+S_AY = S_WX + 16
 S_AC = S_AY + 3
 S_B = S_AC + 4
 S_H = S_B + 4
@@ -32,26 +33,10 @@
 N_SEM = S_PY + 1
 
 
-def one_hot(shape, pairs):
-    m = np.zeros(shape, np.float32)
-    for r, c in pairs:
-        m[r, c] = 1.0
-    return m.astype(jnp.bfloat16)
-
-
-def selections():
-    r2, r4, r16 = range(2), range(4), range(16)
-    rows = [(a, z, x, i) for a in r2 for z in r16 for x in r4 for i in r2]
-    return [
-        one_hot((256, 256), [(x * 64 + z * 4 + a * 2 + i, a * 128 + z * 8 + x * 2 + i) for a, z, x, i in rows]),
-        one_hot((256, 256), [(z * 16 + a * 8 + x * 2 + i, x * 64 + z * 4 + a * 2 + i) for a, z, x, i in rows]),
-        one_hot((256, 256), [(a * 128 + z * 8 + x * 2 + i, z * 16 + a * 8 + x * 2 + i) for a, z, x, i in rows]),
-        one_hot((256, 256), [(x * 64 + a * 32 + z * 2 + i, z * 16 + a * 8 + x * 2 + i) for a, z, x, i in rows]),
-        one_hot((256, 256), [(a * 128 + z * 8 + x * 2 + i, x * 64 + a * 32 + z * 2 + i) for a, z, x, i in rows]),
-        one_hot((72, WCOLS), [(j, g * 72 + j) for g in range(8) for j in range(72)]),
-        one_hot((32, 256), [(r, 8 * r + k) for r in range(32) for k in range(8)]),
-        one_hot((256, 32), [(z * 16 + o * 4 + k, z * 2 + o) for z in r16 for o in r2 for k in r4]),
-    ]
+def pick(rows, cols, source):
+    r = lax.broadcasted_iota(jnp.int32, (rows, 1), 0)
+    c = lax.broadcasted_iota(jnp.int32, (rows, cols), 1)
+    return jnp.where(c == source(r), 1.0, 0.0).astype(BF)
 
 
 def dot(a, b):
@@ -71,11 +56,24 @@
 
 
 def kernel(
-    w_in, in_ref, cot_ref, mod_ref, qg_ref, kg_ref, p_x0, p_x1, p_z1, p_z2, p_x2, repeat, sum8, widen,
+    in_hbm, cot_hbm, mod_hbm, qkv_hbm, proj_hbm, qg_hbm, kg_hbm,
     out_ref, ig_ref, pg_ref,
-    order, rows_in, r1, wz, z1, r2, xw, a, bp, bq, bt, bu, hp, hq, ht, hu, zb, r3, xs, r4, px, pxr, pz, pzr, pgs,
-    ss, rs,
+    in_ref, cot_ref, mod_ref, qkv_ref, proj_ref, qg_ref, kg_ref,
+    order, perm, w_in, rows_in, r1, w4, z1, r2, xw, a, bp, bq, bt, bu, hp, hq, ht, hu, zb, r3, xs, r4, px, pxr, pz, pzr, pgs,
+    ss, rs, ls,
 ):
+    fetches = [
+        pltpu.make_async_copy(src, dst, ls.at[i])
+        for i, (src, dst) in enumerate(
+            [
+                (qkv_hbm, qkv_ref), (proj_hbm, proj_ref), (in_hbm, in_ref), (cot_hbm, cot_ref),
+                (mod_hbm, mod_ref), (qg_hbm, qg_ref), (kg_hbm, kg_ref),
+            ]
+        )
+    ]
+    for fetch in fetches:
+        fetch.start()
+
     f, hd, dp = lax.axis_index("frame"), lax.axis_index("head"), lax.axis_index("dp")
     z, x = f // NX, lax.rem(f, NX)
     core, y = lax.rem(hd, 2), (hd // 2) * 2 + dp
@@ -87,6 +85,9 @@
     def at_x_far(d):
         return (z * NX + mod(x + d, NX), far_hd, dp)
 
+    def at_zx(dz, dx):
+        return (mod(z + dz, NZ) * NX + mod(x + dx, NX), hd, dp)
+
     def at_z(d):
         return (mod(z + d, NZ) * NX + x, hd, dp)
 
@@ -146,6 +147,8 @@
         for d in range(1, NX):
             greet(at_x(d))
             greet(at_x_far(d))
+            for dz in (-2, -1, 1, 2):
+                greet(at_zx(dz, d))
         for d in range(1, NY):
             greet(at_y(d))
         greet(across)
@@ -159,48 +162,74 @@
         root = lax.rsqrt(mean(v * v) + 1e-06)
         return v * root, root
 
+    with jax.named_scope("weights"):
+        for fetch in fetches:
+            fetch.wait()
+        eye = pick(18, 18, lambda r: r)
+        blocks = [qkv_ref[w].astype(F32) for w in range(3)] + [dot_nt(eye, proj_ref[...])]
+        w_all = jnp.concatenate([jnp.where(dp == 0, v[:, :144], v[:, 144:]) for v in blocks], axis=1)
+        tail = jnp.concatenate([w_all[16:18, HD * g : HD * g + HD] for g in range(8)], axis=0)
+        w_in[...] = jnp.concatenate([w_all[:16], tail], axis=1).astype(BF)
+
     with jax.named_scope("rows"):
         feature = lax.broadcasted_iota(jnp.int32, (1152, QF), 0)
         col = lax.broadcasted_iota(jnp.int32, (1, QF), 1)
-        last = col - 256
-        from_col = jnp.where(col < 256, (col // 16) * 72 + col % 16, (last // 2) * 72 + 16 + last % 2)
+        b, k = lax.div(col, GF), lax.rem(col, GF)
+        from_col = jnp.where(k < 64, (k >> 4) * 288 + (k & 15), ((k - 64) >> 1) * 288 + 16 + (k & 1)) + b * 72
+        from_col = jnp.where(k < 72, from_col, -100)
         for q in range(4):
             order[q] = jnp.where(feature == from_col + 18 * q, 1.0, 0.0).astype(BF)
+        perm[0] = pick(256, 256, lambda r: ((r >> 1) & 1) * 128 + (r >> 4) * 8 + ((r >> 2) & 3) * 2 + (r & 1))
+        perm[1] = pick(256, 256, lambda r: ((r >> 1) & 15) * 16 + (r >> 6) * 4 + ((r >> 5) & 1) * 2 + (r & 1))
+        perm[2] = pick(256, 256, lambda r: ((r >> 1) & 1) * 128 + ((r >> 2) & 3) * 32 + (r >> 4) * 2 + (r & 1))
+        perm[3] = pick(256, 256, lambda r: ((r >> 1) & 3) * 64 + (r >> 7) * 32 + ((r >> 3) & 15) * 2 + (r & 1))
         normed, _ = normalise()
         hidden_in = (normed * (1.0 + mod_ref[1:2]) + mod_ref[0:1]).astype(BF)
         d_branch = (mod_ref[2:3] * cot_ref[...].astype(F32)).astype(BF)
         quarter = dot(jnp.concatenate([hidden_in, d_branch], axis=0), order[hd]).astype(BF)
-        rows_in[...] = dot(p_x0[...], quarter).astype(BF).reshape(NX, 64, QF)
+        rows_in[...] = dot(perm[0], quarter).astype(BF).reshape(NZ, 16, QF)
 
     with jax.named_scope("greeted"):
-        pl.semaphore_wait(barrier, 25)
+        pl.semaphore_wait(barrier, 37)
+
+    with jax.named_scope("weights_4"):
+        for i, d in enumerate((8, 4, -4)):
+            send(w_in, w4.at[z // 4], S_W4 + i, at_z(d))
+        z_send(lambda k: rows_in.at[k], r2, S_Z1)
+        r2[z] = rows_in[z]
+        w4[z // 4] = w_in[...]
+        for i, d in enumerate((8, 4, -4)):
+            landed(w4.at[mod(z // 4 - d // 4, 4)], S_W4 + i)
+        tail = w4[:, :, WCOLS : WCOLS + HD].reshape(64, HD)
+        tail = jnp.concatenate([tail] * 8, axis=1)
+        pair = (lax.broadcasted_iota(jnp.int32, (64, WCOLS), 0) >> 1) & 7
+        group = lax.div(lax.broadcasted_iota(jnp.int32, (1, WCOLS), 1), HD)
+        tail = jnp.where(pair == group, tail.astype(F32), 0.0).astype(BF)
+        r = lax.broadcasted_iota(jnp.int32, (16, 64), 0)
+        c = lax.broadcasted_iota(jnp.int32, (16, 64), 1)
+        gather = jnp.where(r == (c >> 4) * 2 + (c & 1), 1.0, 0.0).astype(BF)
+        zq = mod(z, 4)
+        xw[x, zq, 0:64] = w4[:, :, 0:WCOLS].reshape(64, WCOLS)
+        xw[x, zq, 64:80] = dot(gather, tail).astype(BF)
+
+    routes = [(dz, dx) for dx in (2, 1, 3, 0) for dz in ((2 if dx % 2 == 0 else -2), 1, -1, 0) if (dz, dx) != (0, 0)]
+    with jax.named_scope("weights_near"):
+        for i, (dz, dx) in enumerate(routes):
+            send(xw.at[x, zq], xw.at[x, zq], S_WX + i, at_zx(dz, dx))
+
+    with jax.named_scope("rows_z"):
+        z_landed(r2, S_Z1)
+        z1[...] = dot(perm[1], r2[...].reshape(256, QF)).astype(BF).reshape(NX, 64, QF)
+        for d in (2, 1, 3):
+            send(z1.at[mod(x + d, NX)], r1.at[x], S_X1 + d - 1, at_x(d))
+        r1[x] = z1[x]
 
     with jax.named_scope("rows_x"):
         for d in range(1, NX):
-            send(rows_in.at[mod(x + d, NX)], r1.at[x], S_X1 + d - 1, at_x(d))
-        z_send(lambda k: w_in, wz, S_WZ)
-        r1[x] = rows_in[x]
-        wz[z] = w_in[...]
-        for d in range(1, NX):
             landed(r1.at[mod(x - d, NX)], S_X1 + d - 1)
-        z1[...] = dot(p_x1[...], r1[...].reshape(256, QF)).astype(BF).reshape(NZ, 16, QF)
-        z_send(lambda k: z1.at[k], r2, S_Z1)
-        r2[z] = z1[z]
-
-    with jax.named_scope("weights_z"):
-        z_landed(wz, S_WZ)
-        xw[x, 0:256] = wz[:, :, 0:WCOLS].reshape(256, WCOLS)
-        tail = dot(wz[:, :, WCOLS : WCOLS + 72].reshape(256, 72), repeat[...])
-        row8 = lax.broadcasted_iota(jnp.int32, (256, WCOLS), 0) % 8
-        group = lax.broadcasted_iota(jnp.int32, (1, WCOLS), 1) // 72
-        tail = jnp.where(row8 == group, tail, 0.0).astype(BF)
-        xw[x, 256:288] = dot(sum8[...], tail).astype(BF)
-        for d in (2, 1, 3):
-            send(xw.at[x], xw.at[x], S_WX + d - 1, at_x(d))
-
-    with jax.named_scope("rows_z"):
-        z_landed(r2, S_Z1)
-        a[core, y] = dot(p_z1[...], r2[...].reshape(256, QF)).astype(BF)
+        for arr in range(2):
+            for k in range(NX):
+                a[core, y, 128 * arr + 32 * k : 128 * arr + 32 * k + 32] = r1[k, 32 * arr : 32 * arr + 32]
         for d in (2, 1, 3):
             send(a.at[core, y], a.at[core, y], S_AY + d - 1, at_y(d))
         send(a.at[core, y], a.at[core, y], S_AC, across)
@@ -219,14 +248,19 @@
 
     with jax.named_scope("project"):
 
+        def weights(q):
+            return xw[q].reshape(QF, WCOLS)
+
         def project(q):
-            w = xw[q]
+            w = weights(q)
             return dot(rows_of(q, 0), w[:, :QKV]), dot(rows_of(q, 1), w[:, QKV:])
 
-        raw, d_att = project(x)
-        for d in (1, 3, 2):
-            q = mod(x - d, NX)
-            landed(xw.at[q], S_WX + d - 1)
+        raw, d_att = jnp.zeros((256, QKV), F32), jnp.zeros((256, 144), F32)
+        for dx in (0, 1, 3, 2):
+            q = mod(x - dx, NX)
+            for i, (dz, dx_of) in enumerate(routes):
+                if dx_of == dx:
+                    landed(xw.at[q, mod(z - dz, 4)], S_WX + i)
             more_raw, more_d = project(q)
             raw, d_att = raw + more_raw, d_att + more_d
         d_att = d_att.astype(BF)
@@ -267,8 +301,22 @@
     with jax.named_scope("branch"):
         both = jnp.concatenate(att, axis=0)
         for q in range(4):
-            spread(q, dot_nt(both, xw[q, :, QKV:]), bp)
+            spread(q, dot_nt(both, weights(q)[:, QKV:]), bp)
         send(bp.at[1 - core], bq, S_B, across)
+
+    def to_y(own, got, total, far, base):
+        landed(got, base)
+        total[...] = (own[core].astype(F32) + got[...].astype(F32)).astype(BF)
+        for d in (2, 1, 3):
+            send(total.at[mod(y + d, NY)], far.at[d - 1], base + d, at_y(d))
+
+    def y_sum(total, far, base):
+        for d in range(1, NY):
+            landed(far.at[d - 1], base + d)
+        s = total[y].astype(F32)
+        for d in range(1, NY):
+            s += far[d - 1].astype(F32)
+        return s
 
     with jax.named_scope("attend_back"):
         d_raw = []
@@ -293,26 +341,11 @@
                 cols_v.append(dv)
             d_raw.append(jnp.concatenate(cols_q + cols_k + cols_v, axis=1))
         d_raw = jnp.concatenate(d_raw, axis=0)
+        to_y(bp, bq, bt, bu, S_B)
         for q in range(4):
-            spread(q, dot_nt(d_raw, xw[q, :, :QKV]), hp)
+            spread(q, dot_nt(d_raw, weights(q)[:, :QKV]), hp)
         send(hp.at[1 - core], hq, S_H, across)
 
-    def to_y(own, got, total, far, base):
-        landed(got, base)
-        total[...] = (own[core].astype(F32) + got[...].astype(F32)).astype(BF)
-        for d in (2, 1, 3):
-            send(total.at[mod(y + d, NY)], far.at[d - 1], base + d, at_y(d))
-
-    def y_sum(total, far, base):
-        for d in range(1, NY):
-            landed(far.at[d - 1], base + d)
-        s = total[y].astype(F32)
-        for d in range(1, NY):
-            s += far[d - 1].astype(F32)
-        return s
-
-    with jax.named_scope("branch_y"):
-        to_y(bp, bq, bt, bu, S_B)
     with jax.named_scope("hidden_y"):
         to_y(hp, hq, ht, hu, S_H)
 
@@ -329,8 +362,8 @@
     with jax.named_scope("back_z"):
         branch = y_sum(bt, bu, S_B)
         hidden = y_sum(ht, hu, S_H)
-        pair = jnp.concatenate([branch.reshape(NZ, 8, QF), hidden.reshape(NZ, 8, QF)], axis=1)
-        zb[...] = pair.astype(BF)
+        both = jnp.concatenate([branch.astype(BF), hidden.astype(BF)], axis=0)
+        zb[...] = dot(perm[2], both).astype(BF).reshape(NZ, 16, QF)
         z_send(lambda k: zb.at[k], r3, S_Z2)
         r3[z] = zb[z]
 
@@ -340,18 +373,20 @@
         s = px[x].astype(F32)
         for d in range(1, NX):
             s += pxr[d - 1].astype(F32)
-        tail = dot(widen[...], s[256:288].astype(BF))
-        row4 = lax.broadcasted_iota(jnp.int32, (256, QF), 0) % 4
-        group = lax.broadcasted_iota(jnp.int32, (1, QF), 1) // 72
-        tail = jnp.where(row4 == group, tail, 0.0)
+        body = jnp.concatenate([s[GF * b : GF * b + 64] for b in range(4)], axis=0)
+        tail = jnp.concatenate([s[GF * b + 64 : GF * b + 72] for b in range(4)], axis=0).astype(BF)
+        widen = pick(256, 32, lambda r: jnp.where((r & 15) < 8, (r >> 4) * 2 + ((r >> 2) & 1), -1))
+        row4 = lax.broadcasted_iota(jnp.int32, (256, 288), 0) & 3
+        group = lax.div(lax.broadcasted_iota(jnp.int32, (1, 288), 1), HD)
+        tail = jnp.where(row4 == group, dot(widen, tail), 0.0)
         tail = tail[:, 0:72] + tail[:, 72:144] + tail[:, 144:216] + tail[:, 216:288]
-        pz[...] = jnp.concatenate([s[0:256], tail], axis=1).astype(BF).reshape(NZ, 16, 360)
-        z_send(lambda k: pz.at[k], pzr, S_PZ)
-        pzr[z] = pz[z]
+        pz[...] = jnp.concatenate([body, tail], axis=1).astype(BF).reshape(NZ, 16, 360)
+        z_send(lambda k: pz.at[lax.rem(k, 4) * 4 + k // 4], pzr, S_PZ)
+        pzr[z] = pz[zq * 4 + z // 4]
 
     with jax.named_scope("back_x"):
         z_landed(r3, S_Z2)
-        xs[...] = dot(p_z2[...], r3[...].reshape(256, QF)).astype(BF).reshape(NX, 64, QF)
+        xs[...] = dot(perm[1], r3[...].reshape(256, QF)).astype(BF).reshape(NX, 64, QF)
         for d in (2, 1, 3):
             to = mod(x + d, NX)
             send(xs.at[to], r4.at[hd, x], S_XF + d, at_x_far(d))
@@ -376,7 +411,7 @@
     with jax.named_scope("results"):
 
         def natural(q):
-            return dot_nt(dot(p_x2[...], r4[q].reshape(256, QF)).astype(BF), order[q])
+            return dot_nt(dot(perm[3], r4[q].reshape(256, QF)).astype(BF), order[q])
 
         total = natural(hd) + natural(far_hd)
         landed(r4.at[hd + 1 - 2 * core], S_OC)
@@ -400,17 +435,10 @@
     dp = lax.axis_index("dp")
     tokens, width = inputs.shape[1:]
 
-    w_half = lax.dynamic_slice_in_dim(qkv_weight, dp * 144, 144, axis=2)
-    w_half = w_half.transpose(1, 0, 2).reshape(18, QKV)
-    p_half = lax.dynamic_slice_in_dim(proj_weight, dp * 144, 144, axis=0).T
-    w_all = jnp.concatenate([w_half, p_half], axis=1)
-    w_in = jnp.concatenate([w_all[:16], w_all[16:].reshape(16, HD)], axis=1)
-
-    consts = [jnp.asarray(m) for m in selections()]
-
     def vm(*shape, dtype=BF):
         return pltpu.VMEM(shape, dtype)
 
+    operands = (inputs[0], cotangent[0], modulation, qkv_weight, proj_weight, q_gain[None], k_gain[None])
     out, ig, pg = pl.pallas_call(
         kernel,
         out_shape=(
@@ -418,16 +446,19 @@
             jax.ShapeDtypeStruct((tokens, width), BF),
             jax.ShapeDtypeStruct((2, 16, 360), F32),
         ),
-        in_specs=[pl.BlockSpec(memory_space=pltpu.VMEM)] * (6 + len(consts)),
+        in_specs=[pl.BlockSpec(memory_space=pl.ANY)] * 7,
         out_specs=[pl.BlockSpec(memory_space=pltpu.VMEM)] * 3,
         scratch_shapes=[
+            *[vm(*v.shape, dtype=v.dtype) for v in operands],
             vm(4, 1152, QF),
+            vm(4, 256, 256),
+            vm(16, WCOLS + HD),
+            vm(NZ, 16, QF),
             vm(NX, 64, QF),
+            vm(4, 16, WCOLS + HD),
             vm(NX, 64, QF),
-            vm(NZ, 16, WCOLS + HD),
             vm(NZ, 16, QF),
-            vm(NZ, 16, QF),
-            vm(NX, QF, WCOLS),
+            vm(NX, 4, GF, WCOLS),
             vm(2, NY, 256, QF),
             vm(2, NY, 128, QF),
             vm(NY, 128, QF),
@@ -441,20 +472,21 @@
             vm(NZ, 16, QF),
             vm(NX, 64, QF),
             vm(4, NX, 64, QF),
-            vm(NX, QF, QF),
-            vm(3, QF, QF),
+            vm(NX, QF, 288),
+            vm(3, QF, 288),
             vm(NZ, 16, 360),
             vm(NZ, 16, 360),
             vm(2, 16, 360, dtype=F32),
             pltpu.SemaphoreType.DMA((N_SEM,)),
             pltpu.SemaphoreType.DMA((N_SEM,)),
+            pltpu.SemaphoreType.DMA((len(operands),)),
         ],
         compiler_params=pltpu.CompilerParams(
-            collective_id=0, has_side_effects=True, vmem_limit_bytes=48 * 1024 * 1024
+            collective_id=0, has_side_effects=True, vmem_limit_bytes=60 * 1024 * 1024
         ),
-    )(w_in, inputs[0], cotangent[0], modulation, q_gain[None], k_gain[None], *consts)
-
-    pg = jnp.concatenate([pg[:, :, :QF], pg[:, :8, QF:].reshape(2, 2, QF)], axis=1)
+    )(*operands)
+
+    pg = jnp.concatenate([pg[:, :, :288], pg[:, :8, 288:].reshape(2, 2, 288)], axis=1)
     pg = lax.dynamic_slice(pg, (0, 0, dp * 144), (2, 18, 144))
     proj_grad = pg.transpose(0, 2, 1).reshape(288, 18)
     return out[None], ig[None], proj_grad

time: 112 us -> 110 us (0.982)
  local copies, waits for them, and re-layouts: 10.9 us -> 4.89 us
  Pallas kernels: 99.8 us -> 103 us
    unnamed x28 -> x7, local copies, waits for them, and re-layouts: 8.89 us -> 3.26 us
    pallas_call x1, Pallas kernels: 99.8 us -> 103 us  [per_device(): pl.pallas_call(kernel, out_shape=(jax.ShapeDtypeStruct((tokens, width), B...]
where the time goes in v3:
time: 110 us; the launch traced here: 109 us
  Pallas kernels  103 us (94%)
  local copies, waits for them, and re-layouts  4.89 us (4%)
    pallas_call x1, Pallas kernels, per_device(): pl.pallas_call(kernel, out_shape=(jax.ShapeDtypeStruct((tokens, width), B...  103 us
    unnamed x7, local copies, waits for them, and re-layouts  3.26 us

profile of v3, /device:TPU:1, one launch (start us, length us, event | category | flops | bytes accessed | tf_op | source)
XLA Modules:
  0.0 109.5 jit_solution(9177034577448668758)
XLA Ops:
  0.6 1.5 %copy.11.proj_hbm = bf16[288,18]{1,0:T(8,128)(2,1)} copy(bf16[288,18]{0,1:T(8,128)(2,1)} %param.10) | data formatting | bytes 20736 | tf_op args[3]
  2.1 103.0 %shard_map.94 = (bf16[128,1152]{1,0:T(8,128)(2,1)}, bf16[128,1152]{1,0:T(8,128)(2,1)}, f32[2,16,360]{2,1,0:T(8,128)}) custom-call(bf16[128,1152]{1,0:T(8,128)(2,1)} %bitcast.11, bf16[128,1152]{1,0:T(8,128)(2,1)} %bitcast.12, f32[3,1152]{1,0:T(4,128)} %mod_hbm.1, bf16[3,18,288]{2,1,0:T(8,128)(2,1)} %qkv_hbm.1, bf16[288,18]{1,0:T(8,128)(2,1)} %copy.11.proj_hbm, ...), custom_call_target="tpu_custom_call" | custom-call | tf_op jit(solution)/shard_map/pallas_call | solution.py:442
  105.1 0.0 copy-start.1
  105.2 0.8 slice.7
  106.0 0.1 reshape.12
  106.1 0.9 fusion.1
  107.0 0.7 reshape.13
  107.7 0.0 copy-done.1
  107.7 0.0 copy-start
  107.7 0.7 copy.15
  108.4 0.4 copy-done
  108.7 0.7 copy.16
  (1 shorter events, 0.0 us)
Async XLA Ops:
  105.1 2.5 %copy-start.1 = (bf16[128,1152]{1,0:T(8,128)(2,1)S(1)}, bf16[128,1152]{1,0:T(8,128)(2,1)}, u32[]{:S(2)}) copy-start(bf16[128,1152]{1,0:T(8,128)(2,1)} %get-tuple-element.6) | copy-start | bytes 884740
  107.7 1.1 copy-start

commit v4 on v3

--- a/solution.py
+++ b/solution.py
@@ -132,6 +132,7 @@
 
         lax.fori_loop(1, NZ, each, 0)
 
+    routes = [(dz, dx) for dx in (1, 3, 0) for dz in (0, 1, -1, -2 if dx == 3 else 2) if (dz, dx) != (0, 0)]
     barrier = pltpu.get_barrier_semaphore()
 
     def greet(dev):
@@ -147,8 +148,9 @@
         for d in range(1, NX):
             greet(at_x(d))
             greet(at_x_far(d))
-            for dz in (-2, -1, 1, 2):
-                greet(at_zx(dz, d))
+        for dz, dx in routes:
+            if dx and dz:
+                greet(at_zx(dz, dx))
         for d in range(1, NY):
             greet(at_y(d))
         greet(across)
@@ -165,8 +167,7 @@
     with jax.named_scope("weights"):
         for fetch in fetches:
             fetch.wait()
-        eye = pick(18, 18, lambda r: r)
-        blocks = [qkv_ref[w].astype(F32) for w in range(3)] + [dot_nt(eye, proj_ref[...])]
+        blocks = [qkv_ref[w].astype(F32) for w in range(3)] + [proj_ref[...].astype(F32)]
         w_all = jnp.concatenate([jnp.where(dp == 0, v[:, :144], v[:, 144:]) for v in blocks], axis=1)
         tail = jnp.concatenate([w_all[16:18, HD * g : HD * g + HD] for g in range(8)], axis=0)
         w_in[...] = jnp.concatenate([w_all[:16], tail], axis=1).astype(BF)
@@ -190,14 +191,32 @@
         rows_in[...] = dot(perm[0], quarter).astype(BF).reshape(NZ, 16, QF)
 
     with jax.named_scope("greeted"):
-        pl.semaphore_wait(barrier, 37)
-
-    with jax.named_scope("weights_4"):
+        pl.semaphore_wait(barrier, 31)
+
+    zq = mod(z, 4)
+
+    def send_near(lo, hi):
+        for i in range(lo, hi):
+            send(xw.at[x, zq], xw.at[x, zq], S_WX + i, at_zx(*routes[i]))
+
+    def near_landed(dx):
+        for i, (dz, dx_of) in enumerate(routes):
+            if dx_of == dx:
+                landed(xw.at[mod(x - dx, NX), mod(z - dz, 4)], S_WX + i)
+
+    with jax.named_scope("rows_z"):
+        z_send(lambda k: rows_in.at[k], r2, S_Z1)
         for i, d in enumerate((8, 4, -4)):
             send(w_in, w4.at[z // 4], S_W4 + i, at_z(d))
-        z_send(lambda k: rows_in.at[k], r2, S_Z1)
         r2[z] = rows_in[z]
         w4[z // 4] = w_in[...]
+        z_landed(r2, S_Z1)
+        z1[...] = dot(perm[1], r2[...].reshape(256, QF)).astype(BF).reshape(NX, 64, QF)
+        for d in (2, 1, 3):
+            send(z1.at[mod(x + d, NX)], r1.at[x], S_X1 + d - 1, at_x(d))
+        r1[x] = z1[x]
+
+    with jax.named_scope("weights_4"):
         for i, d in enumerate((8, 4, -4)):
             landed(w4.at[mod(z // 4 - d // 4, 4)], S_W4 + i)
         tail = w4[:, :, WCOLS : WCOLS + HD].reshape(64, HD)
@@ -208,21 +227,9 @@
         r = lax.broadcasted_iota(jnp.int32, (16, 64), 0)
         c = lax.broadcasted_iota(jnp.int32, (16, 64), 1)
         gather = jnp.where(r == (c >> 4) * 2 + (c & 1), 1.0, 0.0).astype(BF)
-        zq = mod(z, 4)
         xw[x, zq, 0:64] = w4[:, :, 0:WCOLS].reshape(64, WCOLS)
         xw[x, zq, 64:80] = dot(gather, tail).astype(BF)
-
-    routes = [(dz, dx) for dx in (2, 1, 3, 0) for dz in ((2 if dx % 2 == 0 else -2), 1, -1, 0) if (dz, dx) != (0, 0)]
-    with jax.named_scope("weights_near"):
-        for i, (dz, dx) in enumerate(routes):
-            send(xw.at[x, zq], xw.at[x, zq], S_WX + i, at_zx(dz, dx))
-
-    with jax.named_scope("rows_z"):
-        z_landed(r2, S_Z1)
-        z1[...] = dot(perm[1], r2[...].reshape(256, QF)).astype(BF).reshape(NX, 64, QF)
-        for d in (2, 1, 3):
-            send(z1.at[mod(x + d, NX)], r1.at[x], S_X1 + d - 1, at_x(d))
-        r1[x] = z1[x]
+        send_near(0, 8)
 
     with jax.named_scope("rows_x"):
         for d in range(1, NX):
@@ -234,6 +241,17 @@
             send(a.at[core, y], a.at[core, y], S_AY + d - 1, at_y(d))
         send(a.at[core, y], a.at[core, y], S_AC, across)
 
+    with jax.named_scope("weights_near"):
+        send_near(8, len(routes))
+        near_landed(1)
+        for i, dz in enumerate((0, 1)):
+            slot = xw.at[mod(x - 1, NX), mod(z - dz, 4)]
+            send(slot, slot, S_WX + 11 + i, at_x(1))
+        near_landed(3)
+        for i, dz in enumerate((-1, -2)):
+            slot = xw.at[mod(x + 1, NX), mod(z - dz, 4)]
+            send(slot, slot, S_WX + 13 + i, at_x(-1))
+
     with jax.named_scope("rows_y"):
         for d in (1, 3, 2):
             slot = a.at[core, mod(y - d, NY)]
@@ -256,11 +274,13 @@
             return dot(rows_of(q, 0), w[:, :QKV]), dot(rows_of(q, 1), w[:, QKV:])
 
         raw, d_att = jnp.zeros((256, QKV), F32), jnp.zeros((256, 144), F32)
-        for dx in (0, 1, 3, 2):
+        for dx in (1, 3, 0, 2):
             q = mod(x - dx, NX)
-            for i, (dz, dx_of) in enumerate(routes):
-                if dx_of == dx:
-                    landed(xw.at[q, mod(z - dz, 4)], S_WX + i)
+            if dx == 0:
+                near_landed(0)
+            if dx == 2:
+                for i, dz in enumerate((0, 1, -1, -2)):
+                    landed(xw.at[q, mod(z - dz, 4)], S_WX + 11 + i)
             more_raw, more_d = project(q)
             raw, d_att = raw + more_raw, d_att + more_d
         d_att = d_att.astype(BF)
@@ -346,9 +366,6 @@
             spread(q, dot_nt(d_raw, weights(q)[:, :QKV]), hp)
         send(hp.at[1 - core], hq, S_H, across)
 
-    with jax.named_scope("hidden_y"):
-        to_y(hp, hq, ht, hu, S_H)
-
     with jax.named_scope("proj_grad"):
         none = jnp.zeros((128, 144), BF)
         att_c = jnp.concatenate(
@@ -358,6 +375,9 @@
             px[q] = dot_tn(rows_of(q, 1), att_c).astype(BF)
         for d in (2, 1, 3):
             send(px.at[mod(x + d, NX)], pxr.at[d - 1], S_PX + d - 1, at_x(d))
+
+    with jax.named_scope("hidden_y"):
+        to_y(hp, hq, ht, hu, S_H)
 
     with jax.named_scope("back_z"):
         branch = y_sum(bt, bu, S_B)
@@ -424,7 +444,15 @@
         d_in = root * (d_n - mean(d_n) - normed * mean(d_n * normed))
         ig_ref[...] = (cot_ref[...].astype(F32) + d_in).astype(BF)
         landed(pgs.at[1 - dp], S_PY)
-        pg_ref[...] = pgs[...]
+        halves = []
+        for v in (pgs[0], pgs[1]):
+            last = [
+                jnp.concatenate([jnp.concatenate([v[r + k : r + k + 1, 288:360] for k in range(2)], axis=1) for r in (o, o + 4)], axis=0)
+                for o in (0, 2)
+            ]
+            parts = [jnp.concatenate([v[:, 144 * p : 144 * p + 144], last[p]], axis=0) for p in range(2)]
+            halves.append(jnp.where(dp == 0, parts[0], parts[1]))
+        pg_ref[...] = jnp.concatenate(halves, axis=1)
 
     with jax.named_scope("sent"):
         for wait in sent:
@@ -432,19 +460,18 @@
 
 
 def per_device(inputs, modulation, qkv_weight, proj_weight, q_gain, k_gain, cotangent):
-    dp = lax.axis_index("dp")
     tokens, width = inputs.shape[1:]
 
     def vm(*shape, dtype=BF):
         return pltpu.VMEM(shape, dtype)
 
-    operands = (inputs[0], cotangent[0], modulation, qkv_weight, proj_weight, q_gain[None], k_gain[None])
+    operands = (inputs[0], cotangent[0], modulation, qkv_weight, proj_weight.T, q_gain[None], k_gain[None])
     out, ig, pg = pl.pallas_call(
         kernel,
         out_shape=(
             jax.ShapeDtypeStruct((tokens, width), BF),
             jax.ShapeDtypeStruct((tokens, width), BF),
-            jax.ShapeDtypeStruct((2, 16, 360), F32),
+            jax.ShapeDtypeStruct((18, 288), F32),
         ),
         in_specs=[pl.BlockSpec(memory_space=pl.ANY)] * 7,
         out_specs=[pl.BlockSpec(memory_space=pltpu.VMEM)] * 3,
@@ -486,10 +513,7 @@
         ),
     )(*operands)
 
-    pg = jnp.concatenate([pg[:, :, :288], pg[:, :8, 288:].reshape(2, 2, 288)], axis=1)
-    pg = lax.dynamic_slice(pg, (0, 0, dp * 144), (2, 18, 144))
-    proj_grad = pg.transpose(0, 2, 1).reshape(288, 18)
-    return out[None], ig[None], proj_grad
+    return out[None], ig[None], pg.T
 
 
 def solution(mesh):

time: 110 us -> 99.9 us (0.908)
  Pallas kernels: 103 us -> 95.9 us
  local copies, waits for them, and re-layouts: 4.89 us -> 3.13 us
    pallas_call x1, Pallas kernels: 103 us -> 95.9 us  [per_device(): pl.pallas_call(kernel, out_shape=(jax.ShapeDtypeStruct((tokens, width), B...]
where the time goes in v4:
time: 99.9 us; the launch traced here: 99.7 us
  Pallas kernels  95.9 us (96%)
  local copies, waits for them, and re-layouts  3.13 us (3%)
    pallas_call x1, Pallas kernels, per_device(): pl.pallas_call(kernel, out_shape=(jax.ShapeDtypeStruct((tokens, width), B...  95.9 us
    unnamed x7, local copies, waits for them, and re-layouts  3.13 us

profile of v4, /device:TPU:1, one launch (start us, length us, event | category | flops | bytes accessed | tf_op | source)
XLA Modules:
  0.0 99.7 jit_solution(18235831938873107760)
XLA Ops:
  0.6 95.9 %shard_map.94 = (bf16[128,1152]{1,0:T(8,128)(2,1)}, bf16[128,1152]{1,0:T(8,128)(2,1)}, f32[18,288]{1,0:T(8,128)}) custom-call(bf16[128,1152]{1,0:T(8,128)(2,1)} %bitcast.8, bf16[128,1152]{1,0:T(8,128)(2,1)} %bitcast.9, f32[3,1152]{1,0:T(4,128)} %mod_hbm.1, bf16[3,18,288]{2,1,0:T(8,128)(2,1)} %qkv_hbm.1, bf16[18,288]{1,0:T(8,128)(2,1)} %bitcast.13, ...), custom_call_target="tpu_custom_call" | custom-call | tf_op jit(solution)/shard_map/pallas_call | solution.py:469
  96.5 0.0 copy-start
  96.5 1.7 %copy.13 = bf16[1,128,1152]{2,1,0:T(8,128)(2,1)} copy(bf16[1,128,1152]{2,1,0:T(8,128)(2,1)} %bitcast.11) | data formatting | bytes 589824
  98.3 0.0 copy-done
  98.3 0.0 copy-start.1
  98.3 0.7 copy.14
  99.0 0.1 copy-done.1
  99.1 0.6 copy.15
Async XLA Ops:
  96.5 1.8 %copy-start = (bf16[128,1152]{1,0:T(8,128)(2,1)S(1)}, bf16[128,1152]{1,0:T(8,128)(2,1)}, u32[]{:S(2)}) copy-start(bf16[128,1152]{1,0:T(8,128)(2,1)} %get-tuple-element.7) | copy-start | bytes 884740
  98.3 0.8 copy-start.1

commit v5 on v4

--- a/solution.py
+++ b/solution.py
@@ -132,7 +132,7 @@
 
         lax.fori_loop(1, NZ, each, 0)
 
-    routes = [(dz, dx) for dx in (1, 3, 0) for dz in (0, 1, -1, -2 if dx == 3 else 2) if (dz, dx) != (0, 0)]
+    routes = [(-2, 3), (1, 1), (-1, 3), (0, 1), (2, 1), (0, 3), (-1, 1), (1, 3), (2, 0), (1, 0), (-1, 0)]
     barrier = pltpu.get_barrier_semaphore()
 
     def greet(dev):
@@ -199,10 +199,11 @@
         for i in range(lo, hi):
             send(xw.at[x, zq], xw.at[x, zq], S_WX + i, at_zx(*routes[i]))
 
-    def near_landed(dx):
-        for i, (dz, dx_of) in enumerate(routes):
-            if dx_of == dx:
-                landed(xw.at[mod(x - dx, NX), mod(z - dz, 4)], S_WX + i)
+    def near_landed(i):
+        dz, dx = routes[i]
+        slot = xw.at[mod(x - dx, NX), mod(z - dz, 4)]
+        landed(slot, S_WX + i)
+        return slot
 
     with jax.named_scope("rows_z"):
         z_send(lambda k: rows_in.at[k], r2, S_Z1)
@@ -243,14 +244,9 @@
 
     with jax.named_scope("weights_near"):
         send_near(8, len(routes))
-        near_landed(1)
-        for i, dz in enumerate((0, 1)):
-            slot = xw.at[mod(x - 1, NX), mod(z - dz, 4)]
-            send(slot, slot, S_WX + 11 + i, at_x(1))
-        near_landed(3)
-        for i, dz in enumerate((-1, -2)):
-            slot = xw.at[mod(x + 1, NX), mod(z - dz, 4)]
-            send(slot, slot, S_WX + 13 + i, at_x(-1))
+        for i in range(4):
+            slot = near_landed(i)
+            send(slot, slot, S_WX + 11 + i, at_x(routes[i][1] if routes[i][1] == 1 else -1))
 
     with jax.named_scope("rows_y"):
         for d in (1, 3, 2):
@@ -276,11 +272,12 @@
         raw, d_att = jnp.zeros((256, QKV), F32), jnp.zeros((256, 144), F32)
         for dx in (1, 3, 0, 2):
             q = mod(x - dx, NX)
-            if dx == 0:
-                near_landed(0)
+            for i in range(4, len(routes)):
+                if routes[i][1] == dx:
+                    near_landed(i)
             if dx == 2:
-                for i, dz in enumerate((0, 1, -1, -2)):
-                    landed(xw.at[q, mod(z - dz, 4)], S_WX + 11 + i)
+                for i in range(4):
+                    landed(xw.at[q, mod(z - routes[i][0], 4)], S_WX + 11 + i)
             more_raw, more_d = project(q)
             raw, d_att = raw + more_raw, d_att + more_d
         d_att = d_att.astype(BF)
@@ -338,6 +335,9 @@
             s += far[d - 1].astype(F32)
         return s
 
+    with jax.named_scope("branch_y"):
+        to_y(bp, bq, bt, bu, S_B)
+
     with jax.named_scope("attend_back"):
         d_raw = []
         for p in range(2):
@@ -361,7 +361,6 @@
                 cols_v.append(dv)
             d_raw.append(jnp.concatenate(cols_q + cols_k + cols_v, axis=1))
         d_raw = jnp.concatenate(d_raw, axis=0)
-        to_y(bp, bq, bt, bu, S_B)
         for q in range(4):
             spread(q, dot_nt(d_raw, weights(q)[:, :QKV]), hp)
         send(hp.at[1 - core], hq, S_H, across)
@@ -433,13 +432,13 @@
         def natural(q):
             return dot_nt(dot(perm[3], r4[q].reshape(256, QF)).astype(BF), order[q])
 
+        normed, root = normalise()
         total = natural(hd) + natural(far_hd)
         landed(r4.at[hd + 1 - 2 * core], S_OC)
         total += natural(hd + 1 - 2 * core)
         landed(r4.at[mod(hd + 3 - 2 * core, 4)], S_OC + 1)
         total += natural(mod(hd + 3 - 2 * core, 4))
         out_ref[...] = (in_ref[...].astype(F32) + mod_ref[2:3] * total[0:128]).astype(BF)
-        normed, root = normalise()
         d_n = total[128:256] * (1.0 + mod_ref[1:2])
         d_in = root * (d_n - mean(d_n) - normed * mean(d_n * normed))
         ig_ref[...] = (cot_ref[...].astype(F32) + d_in).astype(BF)

time: 99.9 us -> 97.8 us (0.979)
  Pallas kernels: 95.9 us -> 92.9 us
    pallas_call x1, Pallas kernels: 95.9 us -> 92.9 us  [per_device(): pl.pallas_call(kernel, out_shape=(jax.ShapeDtypeStruct((tokens, width), B...]
where the time goes in v5:
time: 97.8 us; the launch traced here: 96.7 us
  Pallas kernels  92.9 us (95%)
  local copies, waits for them, and re-layouts  3.13 us (3%)
    pallas_call x1, Pallas kernels, per_device(): pl.pallas_call(kernel, out_shape=(jax.ShapeDtypeStruct((tokens, width), B...  92.9 us
    unnamed x7, local copies, waits for them, and re-layouts  3.13 us

profile of v5, /device:TPU:1, one launch (start us, length us, event | category | flops | bytes accessed | tf_op | source)
XLA Modules:
  0.0 96.7 jit_solution(10783542008910382054)
XLA Ops:
  0.6 92.9 %shard_map.94 = (bf16[128,1152]{1,0:T(8,128)(2,1)}, bf16[128,1152]{1,0:T(8,128)(2,1)}, f32[18,288]{1,0:T(8,128)}) custom-call(bf16[128,1152]{1,0:T(8,128)(2,1)} %bitcast.8, bf16[128,1152]{1,0:T(8,128)(2,1)} %bitcast.9, f32[3,1152]{1,0:T(4,128)} %mod_hbm.1, bf16[3,18,288]{2,1,0:T(8,128)(2,1)} %qkv_hbm.1, bf16[18,288]{1,0:T(8,128)(2,1)} %bitcast.13, ...), custom_call_target="tpu_custom_call" | custom-call | tf_op jit(solution)/shard_map/pallas_call | solution.py:468
  93.5 0.0 copy-start
  93.5 1.7 %copy.13 = bf16[1,128,1152]{2,1,0:T(8,128)(2,1)} copy(bf16[1,128,1152]{2,1,0:T(8,128)(2,1)} %bitcast.11) | data formatting | bytes 589824
  95.3 0.0 copy-done
  95.3 0.0 copy-start.1
  95.3 0.7 copy.14
  96.0 0.1 copy-done.1
  96.0 0.6 copy.15
Async XLA Ops:
  93.5 1.8 %copy-start = (bf16[128,1152]{1,0:T(8,128)(2,1)S(1)}, bf16[128,1152]{1,0:T(8,128)(2,1)}, u32[]{:S(2)}) copy-start(bf16[128,1152]{1,0:T(8,128)(2,1)} %get-tuple-element.7) | copy-start | bytes 884740
  95.3 0.8 copy-start.1

commit v6 on v5

--- a/solution.py
+++ b/solution.py
@@ -361,9 +361,11 @@
                 cols_v.append(dv)
             d_raw.append(jnp.concatenate(cols_q + cols_k + cols_v, axis=1))
         d_raw = jnp.concatenate(d_raw, axis=0)
-        for q in range(4):
+        for k in range(4):
+            q = mod(1 - core, 2) + 2 * k if k < 2 else core + 2 * (k - 2)
             spread(q, dot_nt(d_raw, weights(q)[:, :QKV]), hp)
-        send(hp.at[1 - core], hq, S_H, across)
+            if k == 1:
+                send(hp.at[1 - core], hq, S_H, across)
 
     with jax.named_scope("proj_grad"):
         none = jnp.zeros((128, 144), BF)
@@ -451,7 +453,7 @@
             ]
             parts = [jnp.concatenate([v[:, 144 * p : 144 * p + 144], last[p]], axis=0) for p in range(2)]
             halves.append(jnp.where(dp == 0, parts[0], parts[1]))
-        pg_ref[...] = jnp.concatenate(halves, axis=1)
+        pg_ref[0:18, 0:288] = jnp.concatenate(halves, axis=1)
 
     with jax.named_scope("sent"):
         for wait in sent:
@@ -470,7 +472,7 @@
         out_shape=(
             jax.ShapeDtypeStruct((tokens, width), BF),
             jax.ShapeDtypeStruct((tokens, width), BF),
-            jax.ShapeDtypeStruct((18, 288), F32),
+            jax.ShapeDtypeStruct((24, 384), F32),
         ),
         in_specs=[pl.BlockSpec(memory_space=pl.ANY)] * 7,
         out_specs=[pl.BlockSpec(memory_space=pltpu.VMEM)] * 3,
@@ -512,7 +514,7 @@
         ),
     )(*operands)
 
-    return out[None], ig[None], pg.T
+    return out[None], ig[None], pg[:18, :288].T
 
 
 def solution(mesh):

time: 97.8 us -> 97.7 us (level)
    transpose x0 -> x1, local copies, waits for them, and re-layouts: none -> 1.39 us  [per_device(): return (out[None], ig[None], pg[:18, :288].T)]
    unnamed x7 -> x4, local copies, waits for them, and re-layouts: 3.13 us -> 2.46 us
where the time goes in v6:
time: 97.7 us; the launch traced here: 97 us
  Pallas kernels  92.5 us (95%)
  local copies, waits for them, and re-layouts  3.85 us (4%)
    pallas_call x1, Pallas kernels, per_device(): pl.pallas_call(kernel, out_shape=(jax.ShapeDtypeStruct((tokens, width), B...  92.5 us
    unnamed x4, local copies, waits for them, and re-layouts  2.46 us

profile of v6, /device:TPU:1, one launch (start us, length us, event | category | flops | bytes accessed | tf_op | source)
XLA Modules:
  0.0 97.0 jit_solution(6123255040451635428)
XLA Ops:
  0.6 92.5 %shard_map.94 = (bf16[128,1152]{1,0:T(8,128)(2,1)}, bf16[128,1152]{1,0:T(8,128)(2,1)}, f32[24,384]{1,0:T(8,128)}) custom-call(bf16[128,1152]{1,0:T(8,128)(2,1)} %bitcast.9, bf16[128,1152]{1,0:T(8,128)(2,1)} %bitcast.10, f32[3,1152]{1,0:T(4,128)} %mod_hbm.1, bf16[3,18,288]{2,1,0:T(8,128)(2,1)} %qkv_hbm.1, bf16[18,288]{1,0:T(8,128)(2,1)} %bitcast.13, ...), custom_call_target="tpu_custom_call" | custom-call | tf_op jit(solution)/shard_map/pallas_call | solution.py:470
  93.2 1.4 %slice_bitcast_fusion = f32[288,18]{0,1:T(8,128)} fusion(f32[24,384]{1,0:T(8,128)} %get-tuple-element.8), kind=kLoop, calls=%fused_computation | loop fusion | bytes 41472 | tf_op jit(solution)/shard_map/transpose | solution.py:517
  94.6 0.0 copy-start
  94.6 1.7 %copy.12 = bf16[1,128,1152]{2,1,0:T(8,128)(2,1)} copy(bf16[1,128,1152]{2,1,0:T(8,128)(2,1)} %bitcast.12) | data formatting | bytes 589824
  96.3 0.0 copy-done
  96.3 0.7 copy.13
Async XLA Ops:
  94.6 1.7 %copy-start = (bf16[128,1152]{1,0:T(8,128)(2,1)S(1)}, bf16[128,1152]{1,0:T(8,128)(2,1)}, u32[]{:S(2)}) copy-start(bf16[128,1152]{1,0:T(8,128)(2,1)} %get-tuple-element.7) | copy-start | bytes 884740

commit v7 on v6

--- a/solution.py
+++ b/solution.py
@@ -405,6 +405,9 @@
         z_send(lambda k: pz.at[lax.rem(k, 4) * 4 + k // 4], pzr, S_PZ)
         pzr[z] = pz[zq * 4 + z // 4]
 
+    def natural(q):
+        return dot_nt(dot(perm[3], r4[q].reshape(256, QF)).astype(BF), order[q])
+
     with jax.named_scope("back_x"):
         z_landed(r3, S_Z2)
         xs[...] = dot(perm[1], r3[...].reshape(256, QF)).astype(BF).reshape(NX, 64, QF)
@@ -417,9 +420,12 @@
         for d in range(1, NX):
             landed(r4.at[hd, mod(x - d, NX)], S_X2 + d - 1)
         send(r4.at[hd], r4.at[hd], S_OC, across)
+        normed, root = normalise()
+        total = natural(hd)
         for d in range(NX):
             landed(r4.at[far_hd, mod(x - d, NX)], S_XF + d)
         send(r4.at[far_hd], r4.at[far_hd], S_OC + 1, across)
+        total += natural(far_hd)
 
     with jax.named_scope("grad_z"):
         z_landed(pzr, S_PZ)
@@ -430,12 +436,6 @@
         send(pgs.at[dp], pgs.at[dp], S_PY, at_y(1 - 2 * dp))
 
     with jax.named_scope("results"):
-
-        def natural(q):
-            return dot_nt(dot(perm[3], r4[q].reshape(256, QF)).astype(BF), order[q])
-
-        normed, root = normalise()
-        total = natural(hd) + natural(far_hd)
         landed(r4.at[hd + 1 - 2 * core], S_OC)
         total += natural(hd + 1 - 2 * core)
         landed(r4.at[mod(hd + 3 - 2 * core, 4)], S_OC + 1)

time: 97.7 us -> 98.9 us (1.012)
  Pallas kernels: 92.5 us -> 93.9 us
    pallas_call x1, Pallas kernels: 92.5 us -> 93.9 us  [per_device(): pl.pallas_call(kernel, out_shape=(jax.ShapeDtypeStruct((tokens, width), B...]
where the time goes in v7:
time: 98.9 us; the launch traced here: 98.4 us
  Pallas kernels  93.9 us (95%)
  local copies, waits for them, and re-layouts  3.85 us (4%)
    pallas_call x1, Pallas kernels, per_device(): pl.pallas_call(kernel, out_shape=(jax.ShapeDtypeStruct((tokens, width), B...  93.9 us
    unnamed x4, local copies, waits for them, and re-layouts  2.46 us

profile of v7, /device:TPU:1, one launch (start us, length us, event | category | flops | bytes accessed | tf_op | source)
XLA Modules:
  0.0 98.4 jit_solution(1480800744889697414)
XLA Ops:
  0.6 93.9 %shard_map.94 = (bf16[128,1152]{1,0:T(8,128)(2,1)}, bf16[128,1152]{1,0:T(8,128)(2,1)}, f32[24,384]{1,0:T(8,128)}) custom-call(bf16[128,1152]{1,0:T(8,128)(2,1)} %bitcast.9, bf16[128,1152]{1,0:T(8,128)(2,1)} %bitcast.10, f32[3,1152]{1,0:T(4,128)} %mod_hbm.1, bf16[3,18,288]{2,1,0:T(8,128)(2,1)} %qkv_hbm.1, bf16[18,288]{1,0:T(8,128)(2,1)} %bitcast.13, ...), custom_call_target="tpu_custom_call" | custom-call | tf_op jit(solution)/shard_map/pallas_call | solution.py:470
  94.5 1.4 %slice_bitcast_fusion = f32[288,18]{0,1:T(8,128)} fusion(f32[24,384]{1,0:T(8,128)} %get-tuple-element.8), kind=kLoop, calls=%fused_computation | loop fusion | bytes 41472 | tf_op jit(solution)/shard_map/transpose | solution.py:517
  95.9 0.0 copy-start
  95.9 1.7 %copy.12 = bf16[1,128,1152]{2,1,0:T(8,128)(2,1)} copy(bf16[1,128,1152]{2,1,0:T(8,128)(2,1)} %bitcast.12) | data formatting | bytes 589824
  97.7 0.0 copy-done
  97.7 0.7 copy.13
Async XLA Ops:
  95.9 1.7 %copy-start = (bf16[128,1152]{1,0:T(8,128)(2,1)S(1)}, bf16[128,1152]{1,0:T(8,128)(2,1)}, u32[]{:S(2)}) copy-start(bf16[128,1152]{1,0:T(8,128)(2,1)} %get-tuple-element.7) | copy-start | bytes 884740

commit v8 on v6

--- a/solution.py
+++ b/solution.py
@@ -113,11 +113,12 @@
         copy(ref, ref, i, across).wait_recv()
 
     def z_send(src_of, dst, base):
-        def each(d, c):
+        def each(k, c):
+            d = 8 + ((k + 1) // 2) * (1 - 2 * lax.rem(k, 2))
             copy(src_of(mod(z + d, NZ)), dst.at[z], base + d - 1, at_z(d)).start()
             return c
 
-        lax.fori_loop(1, NZ, each, 0)
+        lax.fori_loop(0, NZ - 1, each, 0)
 
         def each_sent(d, c):
             copy(src_of(mod(z + d, NZ)), dst.at[z], base + d - 1, at_z(d)).wait_send()

time: 97.7 us -> 96.8 us (level)
  no operation moved by 1% of the time
where the time goes in v8:
time: 96.8 us; the launch traced here: 96.6 us
  Pallas kernels  92.1 us (95%)
  local copies, waits for them, and re-layouts  3.85 us (4%)
    pallas_call x1, Pallas kernels, per_device(): pl.pallas_call(kernel, out_shape=(jax.ShapeDtypeStruct((tokens, width), B...  92.1 us
    unnamed x4, local copies, waits for them, and re-layouts  2.46 us

profile of v8, /device:TPU:1, one launch (start us, length us, event | category | flops | bytes accessed | tf_op | source)
XLA Modules:
  0.0 96.6 jit_solution(12539106994232774066)
XLA Ops:
  0.6 92.1 %shard_map.94 = (bf16[128,1152]{1,0:T(8,128)(2,1)}, bf16[128,1152]{1,0:T(8,128)(2,1)}, f32[24,384]{1,0:T(8,128)}) custom-call(bf16[128,1152]{1,0:T(8,128)(2,1)} %bitcast.9, bf16[128,1152]{1,0:T(8,128)(2,1)} %bitcast.10, f32[3,1152]{1,0:T(4,128)} %mod_hbm.1, bf16[3,18,288]{2,1,0:T(8,128)(2,1)} %qkv_hbm.1, bf16[18,288]{1,0:T(8,128)(2,1)} %bitcast.13, ...), custom_call_target="tpu_custom_call" | custom-call | tf_op jit(solution)/shard_map/pallas_call | solution.py:471
  92.7 1.4 %slice_bitcast_fusion = f32[288,18]{0,1:T(8,128)} fusion(f32[24,384]{1,0:T(8,128)} %get-tuple-element.8), kind=kLoop, calls=%fused_computation | loop fusion | bytes 41472 | tf_op jit(solution)/shard_map/transpose | solution.py:518
  94.1 0.0 copy-start
  94.1 1.7 %copy.12 = bf16[1,128,1152]{2,1,0:T(8,128)(2,1)} copy(bf16[1,128,1152]{2,1,0:T(8,128)(2,1)} %bitcast.12) | data formatting | bytes 589824
  95.8 0.0 copy-done
  95.8 0.7 copy.13
Async XLA Ops:
  94.1 1.7 %copy-start = (bf16[128,1152]{1,0:T(8,128)(2,1)S(1)}, bf16[128,1152]{1,0:T(8,128)(2,1)}, u32[]{:S(2)}) copy-start(bf16[128,1152]{1,0:T(8,128)(2,1)} %get-tuple-element.7) | copy-start | bytes 884740
